TPU v7x, 256 devices: a whole 4x4x8 slice. The times are simulated.
256 devices in a mesh: seq: 64 (over x, y, z_hi), head: 4 (over z_lo, core).
Axes of the slice: x: 4, y: 4, z: 8 (z_hi: 4, z_lo: 2; z = z_hi * 2 + z_lo), core: 2. Of those that a mesh axis runs over, the one named last changes fastest.
Arguments:
- query: bfloat16 [32768, 4096], P('seq', 'head'), may hold values from -6 to 6
- comp_key: bfloat16 [32768, 1024], P('seq', 'head'), may hold values from -6 to 6
- comp_value: bfloat16 [32768, 1024], P('seq', 'head'), may hold values from -6 to 6
- prompt_key: bfloat16 [2048, 1024], P(('seq', 'head')), may hold values from -6 to 6
- prompt_value: bfloat16 [2048, 1024], P(('seq', 'head')), may hold values from -6 to 6
- out_grad: bfloat16 [32768, 4096], P('seq', 'head'), may hold values from -16 to 16
- row_comp: int32 [32768], P('seq'), may hold values from 0 to 127, as said below
- prompt_owner: int32 [8], replicated, may hold values from 0 to 7, each once
Outputs:
- attn_out: bfloat16 [32768, 4096], P('seq', 'head')
- query_grad: bfloat16 [32768, 4096], P('seq', 'head')
- key_grad: bfloat16 [32768, 1024], P('seq', 'head')
- value_grad: bfloat16 [32768, 1024], P('seq', 'head')
- prompt_key_grad: bfloat16 [2048, 1024], P(('seq', 'head'))
- prompt_value_grad: bfloat16 [2048, 1024], P(('seq', 'head'))
Inputs may be any that keep to these rules, and one draw needn't show every extreme that they name: `row_comp`: each aligned block of 512 rows holds exactly two different completions, each as one run of one or more rows; every completion lies in exactly one block. A permutation: prompt p sits in slot prompt_owner[p].
All inputs are finite; a program needn't handle non-finite values.
Results may differ from a plain program's by a relative error of at most 0.025.
Values may be sent and summed in bfloat16 or wider, within the bound.
A program may use at most 128 MiB of HBM per device.

v0:
```python
import math

import jax
import jax.numpy as jnp
from jax import lax
from jax.sharding import PartitionSpec as P

QH = 32
KVH = 8
HD = 128
NPROMPT = 8
PLEN = 256


NEG_FILL = -1e30


def attend_head(query_part, key_part, value_part, grad_part, visible):
    inv_sqrt = 1.0 / math.sqrt(key_part.shape[-1])
    scores = (
        jnp.einsum("rgd,kd->grk", query_part, key_part, preferred_element_type=jnp.float32)
        * inv_sqrt
    )
    scores = jnp.where(visible[None], scores, NEG_FILL)
    row_max = jnp.max(scores, axis=-1, keepdims=True)
    raw_weights = jnp.exp(scores - row_max)
    weights = raw_weights / jnp.sum(raw_weights, axis=-1, keepdims=True)
    weights_half = weights.astype(jnp.bfloat16)
    attended = jnp.einsum(
        "grk,kd->rgd", weights_half, value_part, preferred_element_type=jnp.float32
    ).astype(jnp.bfloat16)
    row_delta = jnp.sum(grad_part.astype(jnp.float32) * attended.astype(jnp.float32), axis=-1)
    grad_weights = jnp.einsum(
        "rgd,kd->grk", grad_part, value_part, preferred_element_type=jnp.float32
    )
    dscore = weights * (grad_weights - jnp.transpose(row_delta)[..., None])
    dscore_half = dscore.astype(jnp.bfloat16)
    query_grads = (
        jnp.einsum("grk,kd->rgd", dscore_half, key_part, preferred_element_type=jnp.float32)
        * inv_sqrt
    ).astype(jnp.bfloat16)
    key_grads = (
        jnp.einsum("grk,rgd->kd", dscore_half, query_part, preferred_element_type=jnp.float32)
        * inv_sqrt
    )
    value_grads = jnp.einsum(
        "grk,rgd->kd", weights_half, grad_part, preferred_element_type=jnp.float32
    )
    return (attended, query_grads, key_grads, value_grads)


def add_at(running_sum, grad_piece, row_start):
    current = lax.dynamic_slice_in_dim(running_sum, row_start, grad_piece.shape[0], 0)
    return lax.dynamic_update_slice_in_dim(running_sum, current + grad_piece, row_start, 0)


def shards(query, comp_key, comp_value, prompt_key, prompt_value, out_grad, row_comp, prompt_owner):
    row_total = query.shape[0]
    col_width = comp_key.shape[1]
    kv_local = col_width // HD
    q_group = QH // KVH
    seq_count = lax.axis_size("seq")
    full_key, full_value = (
        lax.all_gather(prompt_key, ("seq", "head"), axis=0, tiled=True),
        lax.all_gather(prompt_value, ("seq", "head"), axis=0, tiled=True),
    )
    col_start = lax.axis_index("head") * col_width
    all_key = lax.dynamic_slice_in_dim(full_key, col_start, col_width, 1)
    all_value = lax.dynamic_slice_in_dim(full_value, col_start, col_width, 1)
    prompt_total = all_key.shape[0]
    comp_per_prompt = 2 * seq_count // NPROMPT
    lead_comp = row_comp[0]
    tail_comp = row_comp[row_total - 1]
    owners = jnp.arange(NPROMPT, dtype=jnp.int32)
    lead_slot = jnp.sum(jnp.where(owners == lead_comp // comp_per_prompt, prompt_owner, 0))
    tail_slot = jnp.sum(jnp.where(owners == tail_comp // comp_per_prompt, prompt_owner, 0))
    lead_row = lead_slot * PLEN
    tail_row = tail_slot * PLEN
    key_rows = jnp.concatenate(
        [
            lax.dynamic_slice_in_dim(all_key, lead_row, PLEN, 0),
            lax.dynamic_slice_in_dim(all_key, tail_row, PLEN, 0),
            comp_key,
        ],
        0,
    )
    value_rows = jnp.concatenate(
        [
            lax.dynamic_slice_in_dim(all_value, lead_row, PLEN, 0),
            lax.dynamic_slice_in_dim(all_value, tail_row, PLEN, 0),
            comp_value,
        ],
        0,
    )
    in_lead = row_comp == lead_comp
    positions = jnp.arange(row_total)
    local_seen = (row_comp[:, None] == row_comp[None, :]) & (
        positions[:, None] >= positions[None, :]
    )
    visible = jnp.concatenate(
        [
            jnp.broadcast_to(in_lead[:, None], (row_total, PLEN)),
            jnp.broadcast_to(jnp.logical_not(in_lead)[:, None], (row_total, PLEN)),
            local_seen,
        ],
        1,
    )
    attn_parts = []
    qgrad_parts = []
    kgrad_parts = []
    vgrad_parts = []
    for kv_index in range(kv_local):
        q_lo = kv_index * q_group * HD
        q_hi = q_lo + q_group * HD
        query_part = query[:, q_lo:q_hi].reshape(row_total, q_group, HD)
        grad_part = out_grad[:, q_lo:q_hi].reshape(row_total, q_group, HD)
        key_part = key_rows[:, kv_index * HD : (kv_index + 1) * HD]
        value_part = value_rows[:, kv_index * HD : (kv_index + 1) * HD]
        attended, query_grads, key_grads, value_grads = attend_head(
            query_part, key_part, value_part, grad_part, visible
        )
        attn_parts.append(attended.reshape(row_total, q_group * HD))
        qgrad_parts.append(query_grads.reshape(row_total, q_group * HD))
        kgrad_parts.append(key_grads)
        vgrad_parts.append(value_grads)
    attn_out = jnp.concatenate(attn_parts, 1)
    query_grad = jnp.concatenate(qgrad_parts, 1)
    key_all = jnp.concatenate(kgrad_parts, 1)
    value_all = jnp.concatenate(vgrad_parts, 1)
    key_grad = key_all[2 * PLEN :].astype(jnp.bfloat16)
    value_grad = value_all[2 * PLEN :].astype(jnp.bfloat16)
    both_grads = jnp.concatenate([key_all[: 2 * PLEN], value_all[: 2 * PLEN]], 1)
    prompt_term = jnp.zeros((prompt_total, 2 * col_width), jnp.float32)
    prompt_term = add_at(prompt_term, both_grads[:PLEN], lead_row)
    prompt_term = add_at(prompt_term, both_grads[PLEN:], tail_row)
    summed = lax.psum_scatter(prompt_term, "seq", scatter_dimension=0, tiled=True)
    key_half = summed[:, :col_width].astype(jnp.bfloat16)
    value_half = summed[:, col_width:].astype(jnp.bfloat16)
    prompt_key_grad, prompt_value_grad = (
        lax.all_to_all(key_half, "head", split_axis=0, concat_axis=1, tiled=True),
        lax.all_to_all(value_half, "head", split_axis=0, concat_axis=1, tiled=True),
    )
    return (attn_out, query_grad, key_grad, value_grad, prompt_key_grad, prompt_value_grad)


def solution(mesh):
    placed = (
        P("seq", "head"),
        P("seq", "head"),
        P("seq", "head"),
        P(("seq", "head"), None),
        P(("seq", "head"), None),
        P("seq", "head"),
        P("seq"),
        P(),
    )
    return jax.shard_map(
        shards,
        mesh=mesh,
        in_specs=placed,
        out_specs=(
            P("seq", "head"),
            P("seq", "head"),
            P("seq", "head"),
            P("seq", "head"),
            P(("seq", "head"), None),
            P(("seq", "head"), None),
        ),
        check_vma=False,
    )
```

profile of v0, /device:TPU:1, one launch (start us, length us, event | category | flops | bytes accessed | tf_op | source)
XLA Modules:
  0.0 707.6 jit_solution(2557816721088777091)
XLA Ops:
  8.7 1.3 fusion.44
  15.3 1.3 fusion.33
  19.0 1.3 fusion.43
  23.9 107.3 %all-gather.5.cloned.1.call-done = bf16[2048,1024]{1,0:T(8,128)(2,1)} async-done(((bf16[8,1024]{1,0:T(8,128)(2,1)}), bf16[2048,1024]{1,0:T(8,128)(2,1)}) %all-gather.5.cloned.1.call-update) | async-done | bytes 4194320 | tf_op jit(solution)/shard_map/all_gather | solution.py:64
  131.2 116.2 %all-gather.3.cloned.1.call-done = bf16[2048,1024]{1,0:T(8,128)(2,1)} async-done(((bf16[8,1024]{1,0:T(8,128)(2,1)}), bf16[2048,1024]{1,0:T(8,128)(2,1)}) %all-gather.3.cloned.1.call-update) | async-done | bytes 4194320 | tf_op jit(solution)/shard_map/all_gather | solution.py:65
  247.3 1.5 fusion.40
  250.1 5.2 fusion.45
  255.2 4.7 fusion.15
  260.0 1.4 convolution_bitcast_fusion
  261.5 1.6 multiply_reduce_fusion
  263.1 1.3 fusion.3
  264.4 2.0 copy-done.1
  266.4 1.5 fusion.18
  267.9 6.1 fusion.46
  274.0 4.6 fusion.14
  278.6 1.6 multiply_reduce_fusion.1
  280.2 1.5 convolution_bitcast_fusion.1
  282.4 1.3 fusion.5
  283.8 1.5 fusion.19
  285.7 2.4 broadcast_in_dim.53
  289.0 2.0 fusion.30
  291.0 5.4 copy.122
  296.4 2.9 fusion.17
  300.4 2.1 copy.82
  302.5 2.9 fusion.16
  306.4 1.3 copy.81
  307.7 2.3 pad_maximum_fusion.3
  311.1 322.5 %reduce-scatter.4.cloned.1.call-done = f32[32,512]{1,0:T(8,128)} async-done(((f32[2048,512]{1,0:T(8,128)}), f32[32,512]{1,0:T(8,128)}) %reduce-scatter.4.cloned.1.call-update) | async-done | bytes 65552 | tf_op jit(solution)/shard_map/reduce_scatter | solution.py:136
  635.1 54.5 %all-to-all-start.1 = ((bf16[4,8,256]{2,1,0:T(8,128)(2,1)}), bf16[4,8,256]{2,1,0:T(8,128)(2,1)S(1)}, u32[]{:S(2)}, u32[]{:S(2)}) async-start(bf16[4,8,256]{2,1,0:T(8,128)(2,1)} %get-tuple-element.36), calls=%async_computation.1 | async-start | bytes 32768 | tf_op jit(solution)/shard_map/all_to_all | solution.py:141
  689.7 3.1 all-to-all-done.1
  692.8 4.0 all-to-all-start
  698.4 1.4 all-to-all-done
  (64 shorter events, 17.1 us)
Async XLA Ops:
  7.2 15.1 %copy-start.6 = (bf16[512,1024]{1,0:T(8,128)(2,1)S(1)}, bf16[512,1024]{1,0:T(8,128)(2,1)}, u32[]{:S(2)}) copy-start(bf16[512,1024]{1,0:T(8,128)(2,1)} %param.13) | copy-start | bytes 3145732
  7.2 124.0 %all-gather.5.cloned.1.call-start = ((), (), s32[]{:S(2)}) async-start(), calls=%async_computation.4 | async-start | bytes 4210688 | tf_op jit(solution)/shard_map/all_gather | solution.py:64
  7.9 239.4 %all-gather.3.cloned.1.call-start = ((), (), s32[]{:S(2)}) async-start(), calls=%async_computation.3 | async-start | bytes 4210688 | tf_op jit(solution)/shard_map/all_gather | solution.py:65
  8.7 625.0 %reduce-scatter.4.cloned.1.call-start = ((), (), s32[]{:S(2)}) async-start(), calls=%async_computation.5 | async-start | bytes 4259840 | tf_op jit(solution)/shard_map/reduce_scatter | solution.py:136
  19.0 3.9 copy-start.12
  22.4 227.7 %copy-start.9 = (bf16[512,512]{0,1:T(8,128)(2,1)S(1)}, bf16[512,512]{0,1:T(8,128)(2,1)}, u32[]{:S(2)}) copy-start(bf16[512,512]{0,1:T(8,128)(2,1)} %copy.127) | copy-start | bytes 1572868
  23.8 231.4 %copy-start.11 = (pred[512,1024]{0,1:T(8,128)(4,1)}, pred[512,1024]{0,1:T(8,128)(4,1)S(1)}, u32[]{:S(2)}) copy-start(pred[512,1024]{0,1:T(8,128)(4,1)S(1)} %pad_add_fusion) | copy-start | bytes 1572868
  255.2 7.9 %slice-start = ((s8[8388608]{0:T(1024)(128)(4,1)}), s8[4194304]{0:T(1024)(128)(4,1)S(1)}, s32[]{:S(2)}) async-start(s8[8388608]{0:T(1024)(128)(4,1)} %bitcast.141), calls=%async_computation.6 | async-start | bytes 8388608
  260.0 3.1 slice-start.1
  261.5 17.1 %copy-start.4 = (bf16[1024,256]{0,1:T(8,128)(2,1)}, bf16[1024,256]{0,1:T(8,128)(2,1)S(1)}, u32[]{:S(2)}) copy-start(bf16[1024,256]{0,1:T(8,128)(2,1)S(1)} %pad_maximum_fusion.4) | copy-start | bytes 1572868
  263.1 3.3 copy-start.10
  264.4 2.0 copy-start.1
  266.4 1.5 copy-start.7
  278.6 3.6 copy-start
  280.2 2.3 copy-start.5
  282.4 1.3 copy-start.8
  283.7 1.9 copy-start.2
  305.4 4.6 copy-start.3
  635.1 57.7 %all-to-all-start.1 = ((bf16[4,8,256]{2,1,0:T(8,128)(2,1)}), bf16[4,8,256]{2,1,0:T(8,128)(2,1)S(1)}, u32[]{:S(2)}, u32[]{:S(2)}) async-start(bf16[4,8,256]{2,1,0:T(8,128)(2,1)} %get-tuple-element.36), calls=%async_computation.1 | async-start | bytes 32768 | tf_op jit(solution)/shard_map/all_to_all | solution.py:141
  692.8 7.1 %all-to-all-start = ((bf16[4,8,256]{2,1,0:T(8,128)(2,1)}), bf16[4,8,256]{2,1,0:T(8,128)(2,1)S(1)}, u32[]{:S(2)}, u32[]{:S(2)}) async-start(bf16[4,8,256]{2,1,0:T(8,128)(2,1)} %get-tuple-element.37), calls=%async_computation | async-start | bytes 32768 | tf_op jit(solution)/shard_map/all_to_all | solution.py:140
Sparse Core Ops, SparseCore 0:
  11.7 119.3 all-gather.4
  134.9 112.3 all-gather.2
  296.5 337.0 reduce-scatter.3
where the time goes:
time: 708 us
  waiting for transfers between devices  552 us (78%)
  starting transfers between devices  58.6 us (8%)
  local copies, waits for them, and re-layouts  28.8 us (4%)
  matrix products  28.7 us (4%)
  between operations  20.6 us (3%)
  other arithmetic  18.9 us (3%)
    reduce_scatter x1, waiting for transfers between devices, shards(): lax.psum_scatter(prompt_term, 'seq', scatter_dimension=0, tiled=True)  323 us
    all_gather x1, waiting for transfers between devices, shards(): lax.all_gather(prompt_value, ('seq', 'head'), axis=0, tiled=True)  116 us
    all_gather x1, waiting for transfers between devices, shards(): lax.all_gather(prompt_key, ('seq', 'head'), axis=0, tiled=True)  107 us
    all_to_all x1, starting transfers between devices, shards(): lax.all_to_all(value_half, 'head', split_axis=0, concat_axis=1, tiled=True)  54.5 us
    unnamed x40, local copies, waits for them, and re-layouts  14.8 us
  transfers between devices with their start and end apart: 5, of which 5 were waited for; matrix products, arithmetic and copies ran while one was open for 4% of the time, Pallas kernels for 0%

commit v1 on v0

v1 whole, which is shorter than its diff:
```python
import functools
import math

import jax
import jax.numpy as jnp
from jax import lax
from jax.experimental import pallas as pl
from jax.experimental.pallas import tpu as pltpu
from jax.sharding import PartitionSpec as P

QH = 32
KVH = 8
HD = 128
NPROMPT = 8
PLEN = 256
NGEN = 16
ROWS = 512
GROUP = QH // KVH
HEADS = 4
PLANE = 16
DEPTH = 4
COLS = 256
CHUNK = 128
MESH = pl.DeviceIdType.MESH
INV_SQRT = 1.0 / math.sqrt(HD)
EXP2_SCALE = INV_SQRT * math.log2(math.e)
NEG_FILL = -1e30
F32 = jnp.float32
BF16 = jnp.bfloat16


def place():
    seq = lax.axis_index("seq")
    head = lax.axis_index("head")
    plane = seq // DEPTH
    z = lax.rem(seq, DEPTH)
    unit = 4 * lax.rem(seq, 8) + head
    return seq, head, plane, z, seq // 8, unit


def spread_target(unit, i):
    return (unit // 2) * DEPTH + lax.rem(i, DEPTH), i // DEPTH


def holder_of(plane, i):
    unit = 2 * plane + lax.rem(i, 2)
    return 8 * (i // 2) + unit // 4, lax.rem(unit, 4)


def entry_barrier(peers, spreads):
    seq, head, plane, z, slot, unit = place()
    barrier = pltpu.get_barrier_semaphore()

    def greet_peer(i, carry):
        other = lax.rem(plane + i, PLANE) * DEPTH + z
        pl.semaphore_signal(barrier, inc=1, device_id=(other, head), device_id_type=MESH)
        return carry

    def greet(i, carry):
        for other, other_head in (spread_target(unit, i), holder_of(plane, i)):
            @pl.when(jnp.logical_or(other != seq, other_head != head))
            def _():
                pl.semaphore_signal(barrier, inc=1, device_id=(other, other_head), device_id_type=MESH)
        return carry

    lax.fori_loop(1, PLANE, greet_peer, 0)
    lax.fori_loop(0, 16, greet, 0)
    own = unit // 2 == plane

    @pl.when(own)
    def _():
        pl.semaphore_wait(barrier, 15 + 30)

    @pl.when(jnp.logical_not(own))
    def _():
        pl.semaphore_wait(barrier, 15 + 32)


def wait_bytes(ref, sem):
    pltpu.make_async_copy(ref, ref, sem).wait()


def gather_kernel(
    owner_ref, comp_ref, key_ref, value_ref, out_ref, slots_ref,
    own_rows, dense, packed, picked, info, infos, infos_smem,
    send_a, recv_a, send_i, recv_i, send_b, recv_b, local_sem,
):
    seq, head, plane, z, slot, unit = place()
    entry_barrier(True, True)

    lead = owner_ref[comp_ref[0] // NGEN]
    tail = owner_ref[comp_ref[ROWS - 1] // NGEN]
    row = lax.broadcasted_iota(jnp.int32, (8, 128), 0)
    info[...] = jnp.where(row < 4, lead, tail)
    infos[plane] = info[...]

    both = jnp.concatenate([key_ref[...].astype(F32), value_ref[...].astype(F32)], 0).astype(BF16)
    for part in range(HEADS):
        own_rows[part] = both[:, part * COLS : (part + 1) * COLS]

    def copy_a(i):
        other, other_head = spread_target(unit, i)
        is_self = jnp.logical_and(other == seq, other_head == head)
        copy = pltpu.make_async_remote_copy(
            src_ref=own_rows.at[i // DEPTH], dst_ref=dense.at[2 * slot + lax.rem(unit, 2)],
            send_sem=send_a.at[i], recv_sem=recv_a.at[2 * slot + lax.rem(unit, 2)],
            device_id=(other, other_head), device_id_type=MESH,
        )
        return is_self, copy

    def start_a(i, carry):
        is_self, copy = copy_a(i)

        @pl.when(is_self)
        def _():
            pltpu.make_async_copy(
                own_rows.at[i // DEPTH], dense.at[2 * slot + lax.rem(unit, 2)],
                recv_a.at[2 * slot + lax.rem(unit, 2)],
            ).start()

        @pl.when(jnp.logical_not(is_self))
        def _():
            copy.start()

        return carry

    def copy_info(i):
        other = lax.rem(plane + i, PLANE)
        return pltpu.make_async_remote_copy(
            src_ref=info, dst_ref=infos.at[plane],
            send_sem=send_i.at[i], recv_sem=recv_i.at[plane],
            device_id=(other * DEPTH + z, head), device_id_type=MESH,
        )

    def start_info(i, carry):
        copy_info(i).start()
        return carry

    lax.fori_loop(1, PLANE, start_info, 0)
    lax.fori_loop(0, 16, start_a, 0)

    def wait_info(i, carry):
        other = lax.rem(plane + i, PLANE)
        wait_bytes(infos.at[other], recv_i.at[other])
        return carry

    lax.fori_loop(1, PLANE, wait_info, 0)
    to_smem = pltpu.make_async_copy(infos, infos_smem, local_sem)
    to_smem.start()

    def wait_a(i, carry):
        wait_bytes(dense.at[i], recv_a.at[i])
        return carry

    lax.fori_loop(0, 16, wait_a, 0)
    to_smem.wait()
    for p in range(NPROMPT):
        first = dense[2 * p].astype(F32)
        second = dense[2 * p + 1].astype(F32)
        packed[p, 0] = jnp.concatenate([first[:8], second[:8]], 0).astype(BF16)
        packed[p, 1] = jnp.concatenate([first[8:], second[8:]], 0).astype(BF16)

    def copy_b(i):
        other = lax.rem(plane + i, PLANE)
        return pltpu.make_async_remote_copy(
            src_ref=picked.at[i], dst_ref=out_ref.at[plane],
            send_sem=send_b.at[i], recv_sem=recv_b.at[plane],
            device_id=(other * DEPTH + z, head), device_id_type=MESH,
        )

    def start_b(i, carry):
        other = lax.rem(plane + i, PLANE)
        picked[i, 0] = packed[infos_smem[other, 0, 0]]
        picked[i, 1] = packed[infos_smem[other, 4, 0]]
        copy_b(i).start()
        return carry

    lax.fori_loop(1, PLANE, start_b, 0)
    out_ref[plane, 0] = packed[lead]
    out_ref[plane, 1] = packed[tail]

    def note_slot(i, carry):
        slots_ref[2 * i] = infos_smem[i, 0, 0]
        slots_ref[2 * i + 1] = infos_smem[i, 4, 0]
        return carry

    lax.fori_loop(0, PLANE, note_slot, 0)

    def wait_b(i, carry):
        other = lax.rem(plane + i, PLANE)
        wait_bytes(out_ref.at[other], recv_b.at[other])
        return carry

    lax.fori_loop(1, PLANE, wait_b, 0)

    def wait_sends(i, carry):
        copy_info(i).wait_send()
        copy_b(i).wait_send()
        return carry

    lax.fori_loop(1, PLANE, wait_sends, 0)

    def wait_send_a(i, carry):
        is_self, copy = copy_a(i)

        @pl.when(jnp.logical_not(is_self))
        def _():
            copy.wait_send()

        return carry

    lax.fori_loop(0, 16, wait_send_a, 0)


def reduce_kernel(
    slots_ref, part_ref, key_out, value_out,
    parts, pieces, finals, send_b, recv_b, send_a, recv_a,
):
    seq, head, plane, z, slot, unit = place()
    entry_barrier(True, True)

    def copy_b(i):
        other = lax.rem(plane + i, PLANE)
        return pltpu.make_async_remote_copy(
            src_ref=part_ref.at[other], dst_ref=parts.at[plane],
            send_sem=send_b.at[i], recv_sem=recv_b.at[plane],
            device_id=(other * DEPTH + z, head), device_id_type=MESH,
        )

    def start_b(i, carry):
        copy_b(i).start()
        return carry

    lax.fori_loop(1, PLANE, start_b, 0)
    parts[plane] = part_ref[plane]

    lane = lax.broadcasted_iota(jnp.int32, (1, 2 * PLANE * 16), 1)
    lane_slot = jnp.zeros((1, 2 * PLANE * 16), jnp.int32)
    for i in range(2 * PLANE):
        lane_slot = jnp.where(lane // 16 == i, slots_ref[i], lane_slot)
    row = lax.broadcasted_iota(jnp.int32, (NPROMPT * 16, 2 * PLANE * 16), 0)
    lanes = lax.broadcasted_iota(jnp.int32, (NPROMPT * 16, 2 * PLANE * 16), 1)
    chosen = jnp.logical_and(row // 16 == lane_slot, lax.rem(row, 16) == lax.rem(lanes, 16))
    chosen = jnp.where(chosen, 1.0, 0.0).astype(BF16)

    def wait_b(i, carry):
        other = lax.rem(plane + i, PLANE)
        wait_bytes(parts.at[other], recv_b.at[other])
        return carry

    lax.fori_loop(1, PLANE, wait_b, 0)
    sums = [
        jnp.dot(chosen, parts[:, :, kv].reshape(2 * PLANE * 16, COLS), preferred_element_type=F32)
        for kv in range(2)
    ]
    for p in range(NPROMPT):
        for k in range(2):
            lo = 16 * p + 8 * k
            pieces[2 * p + k] = jnp.concatenate([sums[0][lo : lo + 8], sums[1][lo : lo + 8]], 0).astype(BF16)

    def copy_a(i):
        other, other_head = holder_of(plane, i)
        is_self = jnp.logical_and(other == seq, other_head == head)
        copy = pltpu.make_async_remote_copy(
            src_ref=pieces.at[i], dst_ref=finals.at[DEPTH * head + z],
            send_sem=send_a.at[i], recv_sem=recv_a.at[DEPTH * head + z],
            device_id=(other, other_head), device_id_type=MESH,
        )
        return is_self, copy

    def start_a(i, carry):
        is_self, copy = copy_a(i)

        @pl.when(is_self)
        def _():
            pltpu.make_async_copy(
                pieces.at[i], finals.at[DEPTH * head + z], recv_a.at[DEPTH * head + z]
            ).start()

        @pl.when(jnp.logical_not(is_self))
        def _():
            copy.start()

        return carry

    lax.fori_loop(0, 16, start_a, 0)

    def wait_a(i, carry):
        wait_bytes(finals.at[i], recv_a.at[i])
        return carry

    lax.fori_loop(0, 16, wait_a, 0)
    for part in range(HEADS):
        total = finals[DEPTH * part].astype(F32)
        for other_z in range(1, DEPTH):
            total = total + finals[DEPTH * part + other_z].astype(F32)
        key_out[:, part * COLS : (part + 1) * COLS] = total[:8].astype(BF16)
        value_out[:, part * COLS : (part + 1) * COLS] = total[8:].astype(BF16)

    def wait_sends(i, carry):
        copy_b(i).wait_send()
        return carry

    lax.fori_loop(1, PLANE, wait_sends, 0)

    def wait_send_a(i, carry):
        is_self, copy = copy_a(i)

        @pl.when(jnp.logical_not(is_self))
        def _():
            copy.wait_send()

        return carry

    lax.fori_loop(0, 16, wait_send_a, 0)


def dot(a, b):
    return jnp.dot(a, b, preferred_element_type=F32)


def attend_kernel(
    comp_ref, q_ref, k_ref, v_ref, kv_ref, g_ref,
    out_ref, qg_ref, kg_ref, vg_ref, part_ref,
    w_prompt, d_prompt, w_local, d_local,
):
    lead_rows = comp_ref[...] == comp_ref[0, 0]
    split = jnp.sum(jnp.where(lead_rows, 1.0, 0.0)).astype(jnp.int32)
    key_pair = jnp.concatenate([kv_ref[:, t, 0].reshape(PLEN, HD) for t in range(2)], 1)
    value_pair = jnp.concatenate([kv_ref[:, t, 1].reshape(PLEN, HD) for t in range(2)], 1)
    key_pair_t = key_pair.T
    value_pair_t = value_pair.T
    keys_t = k_ref[...].T
    values_t = v_ref[...].T
    for chunk in range(ROWS // CHUNK):
        lo, hi = chunk * CHUNK, (chunk + 1) * CHUNK
        span = slice(chunk * GROUP * CHUNK, (chunk + 1) * GROUP * CHUNK)
        q_t = jnp.concatenate([q_ref[lo:hi, j * HD : (j + 1) * HD].T for j in range(GROUP)], 1)
        g_t = jnp.concatenate([g_ref[lo:hi, j * HD : (j + 1) * HD].T for j in range(GROUP)], 1)
        row = lo + lax.broadcasted_iota(jnp.int32, (1, GROUP * CHUNK), 1) % CHUNK
        is_lead = row < split
        zero = jnp.zeros_like(q_t)
        q_pair_t = jnp.concatenate([jnp.where(is_lead, q_t, zero), jnp.where(is_lead, zero, q_t)], 0)
        g_pair_t = jnp.concatenate([jnp.where(is_lead, g_t, zero), jnp.where(is_lead, zero, g_t)], 0)
        key_at = lax.broadcasted_iota(jnp.int32, (hi, CHUNK), 0)
        row_at = lo + lax.broadcasted_iota(jnp.int32, (hi, CHUNK), 1)
        seen = jnp.logical_and(key_at <= row_at, jnp.logical_or(key_at >= split, row_at < split))
        bias = jnp.where(seen, 0.0, NEG_FILL)
        bias = jnp.concatenate([bias] * GROUP, 1)
        s_prompt = dot(key_pair, q_pair_t)
        s_local = dot(k_ref[:hi], q_t) + bias
        top = jnp.maximum(
            jnp.max(s_prompt, axis=0, keepdims=True), jnp.max(s_local, axis=0, keepdims=True)
        )
        e_prompt = jnp.exp2((s_prompt - top) * EXP2_SCALE)
        e_local = jnp.exp2((s_local - top) * EXP2_SCALE)
        total = jnp.sum(e_prompt, axis=0, keepdims=True) + jnp.sum(e_local, axis=0, keepdims=True)
        inv = 1.0 / total
        e_prompt = e_prompt * inv
        e_local = e_local * inv
        wh_prompt = e_prompt.astype(BF16)
        wh_local = e_local.astype(BF16)
        w_prompt[:, span] = wh_prompt
        w_local[:hi, span] = wh_local
        o_pair = dot(value_pair_t, wh_prompt)
        o_t = jnp.where(is_lead, o_pair[:HD], o_pair[HD:]) + dot(values_t[:, :hi], wh_local)
        o_t = o_t.astype(BF16).astype(F32)
        delta = jnp.sum(o_t * g_t.astype(F32), axis=0, keepdims=True)
        ds_prompt = (e_prompt * (dot(value_pair, g_pair_t) - delta)).astype(BF16)
        ds_local = (e_local * (dot(v_ref[:hi], g_t) - delta)).astype(BF16)
        d_prompt[:, span] = ds_prompt
        d_local[:hi, span] = ds_local
        dq_pair = dot(key_pair_t, ds_prompt)
        dq_t = jnp.where(is_lead, dq_pair[:HD], dq_pair[HD:]) + dot(keys_t[:, :hi], ds_local)
        dq_t = dq_t * INV_SQRT
        for j in range(GROUP):
            out_ref[lo:hi, j * HD : (j + 1) * HD] = o_t[:, j * CHUNK : (j + 1) * CHUNK].T.astype(BF16)
            qg_ref[lo:hi, j * HD : (j + 1) * HD] = dq_t[:, j * CHUNK : (j + 1) * CHUNK].T.astype(BF16)

    def stacked(ref):
        return jnp.concatenate(
            [
                ref[c * CHUNK : (c + 1) * CHUNK, j * HD : (j + 1) * HD]
                for c in range(ROWS // CHUNK)
                for j in range(GROUP)
            ],
            0,
        )

    q_all = stacked(q_ref)
    g_all = stacked(g_ref)
    at = lax.broadcasted_iota(jnp.int32, (GROUP * ROWS, 1), 0)
    in_lead = (at // (GROUP * CHUNK)) * CHUNK + at % CHUNK < split
    zeros = jnp.zeros_like(q_all)
    q_pair = jnp.concatenate([jnp.where(in_lead, q_all, zeros), jnp.where(in_lead, zeros, q_all)], 1)
    g_pair = jnp.concatenate([jnp.where(in_lead, g_all, zeros), jnp.where(in_lead, zeros, g_all)], 1)
    dk_pair = dot(d_prompt[...], q_pair) * INV_SQRT
    dv_pair = dot(w_prompt[...], g_pair)
    for t in range(2):
        part_ref[:, t, 0] = dk_pair[:, t * HD : (t + 1) * HD].astype(BF16).reshape(16, 16, HD)
        part_ref[:, t, 1] = dv_pair[:, t * HD : (t + 1) * HD].astype(BF16).reshape(16, 16, HD)
    for chunk in range(ROWS // CHUNK):
        lo, hi = chunk * CHUNK, (chunk + 1) * CHUNK
        start = chunk * GROUP * CHUNK
        kg_ref[lo:hi] = (dot(d_local[lo:hi, start:], q_all[start:]) * INV_SQRT).astype(BF16)
        vg_ref[lo:hi] = dot(w_local[lo:hi, start:], g_all[start:]).astype(BF16)


def shards(query, comp_key, comp_value, prompt_key, prompt_value, out_grad, row_comp, prompt_owner):
    vmem = pl.BlockSpec(memory_space=pltpu.VMEM)
    smem = pl.BlockSpec(memory_space=pltpu.SMEM)
    dma = pltpu.SemaphoreType.DMA
    selected, slots = pl.pallas_call(
        gather_kernel,
        out_shape=(
            jax.ShapeDtypeStruct((PLANE, 2, 2, 16, COLS), BF16),
            jax.ShapeDtypeStruct((2 * PLANE,), jnp.int32),
        ),
        in_specs=[smem, smem, vmem, vmem],
        out_specs=(vmem, smem),
        scratch_shapes=[
            pltpu.VMEM((HEADS, 16, COLS), BF16),
            pltpu.VMEM((16, 16, COLS), BF16),
            pltpu.VMEM((NPROMPT, 2, 16, COLS), BF16),
            pltpu.VMEM((PLANE, 2, 2, 16, COLS), BF16),
            pltpu.VMEM((8, 128), jnp.int32),
            pltpu.VMEM((PLANE, 8, 128), jnp.int32),
            pltpu.SMEM((PLANE, 8, 128), jnp.int32),
            dma((16,)), dma((16,)), dma((16,)), dma((16,)), dma((16,)), dma((16,)), dma,
        ],
        compiler_params=pltpu.CompilerParams(collective_id=0, has_side_effects=True),
        name="gather",
    )(prompt_owner, row_comp, prompt_key, prompt_value)

    kv_local = COLS // HD
    wide = GROUP * HD
    attn_out, query_grad, key_grad, value_grad, parts = pl.pallas_call(
        attend_kernel,
        grid=(kv_local,),
        out_shape=(
            jax.ShapeDtypeStruct(query.shape, BF16),
            jax.ShapeDtypeStruct(query.shape, BF16),
            jax.ShapeDtypeStruct(comp_key.shape, BF16),
            jax.ShapeDtypeStruct(comp_key.shape, BF16),
            jax.ShapeDtypeStruct((PLANE, 2, 2, 16, COLS), BF16),
        ),
        in_specs=[
            pl.BlockSpec((4, 128), lambda g: (0, 0)),
            pl.BlockSpec((ROWS, wide), lambda g: (0, g)),
            pl.BlockSpec((ROWS, HD), lambda g: (0, g)),
            pl.BlockSpec((ROWS, HD), lambda g: (0, g)),
            pl.BlockSpec((PLANE, 2, 2, 16, HD), lambda g: (0, 0, 0, 0, g)),
            pl.BlockSpec((ROWS, wide), lambda g: (0, g)),
        ],
        out_specs=(
            pl.BlockSpec((ROWS, wide), lambda g: (0, g)),
            pl.BlockSpec((ROWS, wide), lambda g: (0, g)),
            pl.BlockSpec((ROWS, HD), lambda g: (0, g)),
            pl.BlockSpec((ROWS, HD), lambda g: (0, g)),
            pl.BlockSpec((PLANE, 2, 2, 16, HD), lambda g: (0, 0, 0, 0, g)),
        ),
        scratch_shapes=[
            pltpu.VMEM((PLEN, GROUP * ROWS), BF16),
            pltpu.VMEM((PLEN, GROUP * ROWS), BF16),
            pltpu.VMEM((ROWS, GROUP * ROWS), BF16),
            pltpu.VMEM((ROWS, GROUP * ROWS), BF16),
        ],
        compiler_params=pltpu.CompilerParams(vmem_limit_bytes=48 * 1024 * 1024),
        name="attend",
    )(row_comp.reshape(4, 128), query, comp_key, comp_value, selected, out_grad)

    prompt_key_grad, prompt_value_grad = pl.pallas_call(
        reduce_kernel,
        out_shape=(
            jax.ShapeDtypeStruct(prompt_key.shape, BF16),
            jax.ShapeDtypeStruct(prompt_key.shape, BF16),
        ),
        in_specs=[smem, vmem],
        out_specs=(vmem, vmem),
        scratch_shapes=[
            pltpu.VMEM((PLANE, 2, 2, 16, COLS), BF16),
            pltpu.VMEM((16, 16, COLS), BF16),
            pltpu.VMEM((16, 16, COLS), BF16),
            dma((16,)), dma((16,)), dma((16,)), dma((16,)),
        ],
        compiler_params=pltpu.CompilerParams(collective_id=1, has_side_effects=True),
        name="reduce",
    )(slots, parts)
    return (attn_out, query_grad, key_grad, value_grad, prompt_key_grad, prompt_value_grad)


def solution(mesh):
    placed = (
        P("seq", "head"),
        P("seq", "head"),
        P("seq", "head"),
        P(("seq", "head"), None),
        P(("seq", "head"), None),
        P("seq", "head"),
        P("seq"),
        P(),
    )
    return jax.shard_map(
        shards,
        mesh=mesh,
        in_specs=placed,
        out_specs=(
            P("seq", "head"),
            P("seq", "head"),
            P("seq", "head"),
            P("seq", "head"),
            P(("seq", "head"), None),
            P(("seq", "head"), None),
        ),
        check_vma=False,
    )
```

time: 708 us -> 84.7 us (0.12)
  the two profiles are of different devices: /device:TPU:1 before, /device:TPU:71 now
where the time goes in v1:
time: 84.7 us; the launch traced here: 84.3 us
  Pallas kernels  74.8 us (88%)
  local copies, waits for them, and re-layouts  8.8 us (10%)
    pallas_call x1, Pallas kernels, shards(): pl.pallas_call(reduce_kernel, out_shape=(jax.ShapeDtypeStruct(prompt_key....  35.7 us
    pallas_call x1, Pallas kernels, shards(): pl.pallas_call(gather_kernel, out_shape=(jax.ShapeDtypeStruct((PLANE, 2,...  26.7 us
    pallas_call x1, Pallas kernels, shards(): pl.pallas_call(attend_kernel, grid=(kv_local,), out_shape=(jax.ShapeDtype...  12.5 us
    unnamed x18, local copies, waits for them, and re-layouts  8.8 us

profile of v1, /device:TPU:71, one launch (start us, length us, event | category | flops | bytes accessed | tf_op | source)
XLA Modules:
  0.0 84.3 jit_solution(3251087228835943582)
XLA Ops:
  0.6 26.7 %gather.1 = (bf16[16,2,2,16,256]{4,3,2,1,0:T(8,128)(2,1)}, s32[32]{0:T(128)}) custom-call(s32[8]{0:T(128)} %owner_ref.1, s32[512]{0:T(512)} %comp_ref.1, bf16[8,1024]{1,0:T(8,128)(2,1)} %key_ref.1, bf16[8,1024]{1,0:T(8,128)(2,1)} %value_ref.1), custom_call_target="tpu_custom_call" | custom-call | tf_op jit(solution)/shard_map/gather/pallas_call | solution.py:413
  27.4 0.0 copy-start.6
  27.4 0.7 copy-done.6
  28.0 0.0 copy-start
  28.0 1.2 %copy-done = bf16[512,1024]{1,0:T(8,128)(2,1)S(1)} copy-done((bf16[512,1024]{1,0:T(8,128)(2,1)S(1)}, bf16[512,1024]{1,0:T(8,128)(2,1)}, u32[]{:S(2)}) %copy-start) | copy-done | bytes 1048600
  29.3 0.0 copy-start.1
  29.3 1.2 %copy-done.1 = bf16[512,1024]{1,0:T(8,128)(2,1)S(1)} copy-done((bf16[512,1024]{1,0:T(8,128)(2,1)S(1)}, bf16[512,1024]{1,0:T(8,128)(2,1)}, u32[]{:S(2)}) %copy-start.1) | copy-done | bytes 1048600
  30.5 0.0 copy-start.3
  30.5 1.0 %copy-done.3 = bf16[16,2,2,16,256]{4,3,2,1,0:T(8,128)(2,1)S(1)} copy-done((bf16[16,2,2,16,256]{4,3,2,1,0:T(8,128)(2,1)S(1)}, bf16[16,2,2,16,256]{4,3,2,1,0:T(8,128)(2,1)}, u32[]{:S(2)}) %copy-start.3) | copy-done | bytes 524312
  31.5 0.0 copy-start.4
  31.5 0.9 %copy-done.4 = bf16[512,256]{1,0:T(8,128)(2,1)S(1)} copy-done((bf16[512,256]{1,0:T(8,128)(2,1)S(1)}, bf16[512,256]{1,0:T(8,128)(2,1)}, u32[]{:S(2)}) %copy-start.4) | copy-done | bytes 262168
  32.5 0.0 copy-start.5
  32.5 0.9 %copy-done.5 = bf16[512,256]{1,0:T(8,128)(2,1)S(1)} copy-done((bf16[512,256]{1,0:T(8,128)(2,1)S(1)}, bf16[512,256]{1,0:T(8,128)(2,1)}, u32[]{:S(2)}) %copy-start.5) | copy-done | bytes 262168
  33.4 12.5 %attend.1 = (bf16[512,1024]{1,0:T(8,128)(2,1)}, bf16[512,1024]{1,0:T(8,128)(2,1)}, bf16[512,256]{1,0:T(8,128)(2,1)}, bf16[512,256]{1,0:T(8,128)(2,1)}, bf16[16,2,2,16,256]{4,3,2,1,0:T(8,128)(2,1)S(1)}) custom-call(s32[4,128]{1,0:T(4,128)S(1)} %bitcast.1, bf16[512,1024]{1,0:T(8,128)(2,1)S(1)} %copy-done, bf16[512,256]{1,0:T(8,128)(2,1)S(1)} %copy-done.4, ...), custom_call_target="tpu_custom_call" | custom-call | tf_op jit(solution)/shard_map/attend/pallas_call | solution.py:437
  45.9 0.0 copy-start.2
  45.9 0.8 copy-done.2
  46.7 35.7 %reduce.1 = (bf16[8,1024]{1,0:T(8,128)(2,1)}, bf16[8,1024]{1,0:T(8,128)(2,1)}) custom-call(s32[32]{0:T(128)} %get-tuple-element.20.slots_ref, bf16[16,2,2,16,256]{4,3,2,1,0:T(8,128)(2,1)} %copy-done.2), custom_call_target="tpu_custom_call" | custom-call | tf_op jit(solution)/shard_map/reduce/pallas_call | solution.py:472
  82.4 0.0 copy-start.7
  82.4 1.3 %copy.16 = bf16[8,1024]{1,0:T(8,128)(2,1)} copy(bf16[8,1024]{1,0:T(8,128)(2,1)} %get-tuple-element.34) | data formatting | bytes 32768
  83.7 0.0 copy-done.7
  83.7 0.6 copy.17
Async XLA Ops:
  27.4 0.7 copy-start.6
  28.0 1.2 %copy-start = (bf16[512,1024]{1,0:T(8,128)(2,1)S(1)}, bf16[512,1024]{1,0:T(8,128)(2,1)}, u32[]{:S(2)}) copy-start(bf16[512,1024]{1,0:T(8,128)(2,1)} %q_ref.1) | copy-start | bytes 3145732
  29.3 1.2 %copy-start.1 = (bf16[512,1024]{1,0:T(8,128)(2,1)S(1)}, bf16[512,1024]{1,0:T(8,128)(2,1)}, u32[]{:S(2)}) copy-start(bf16[512,1024]{1,0:T(8,128)(2,1)} %g_ref.1) | copy-start | bytes 3145732
  30.5 1.0 %copy-start.3 = (bf16[16,2,2,16,256]{4,3,2,1,0:T(8,128)(2,1)S(1)}, bf16[16,2,2,16,256]{4,3,2,1,0:T(8,128)(2,1)}, u32[]{:S(2)}) copy-start(bf16[16,2,2,16,256]{4,3,2,1,0:T(8,128)(2,1)} %get-tuple-element.15.kv_ref) | copy-start | bytes 1572868
  31.5 0.9 %copy-start.4 = (bf16[512,256]{1,0:T(8,128)(2,1)S(1)}, bf16[512,256]{1,0:T(8,128)(2,1)}, u32[]{:S(2)}) copy-start(bf16[512,256]{1,0:T(8,128)(2,1)} %k_ref.1) | copy-start | bytes 786436
  32.5 0.9 %copy-start.5 = (bf16[512,256]{1,0:T(8,128)(2,1)S(1)}, bf16[512,256]{1,0:T(8,128)(2,1)}, u32[]{:S(2)}) copy-start(bf16[512,256]{1,0:T(8,128)(2,1)} %v_ref.1) | copy-start | bytes 786436
  45.9 0.8 copy-start.2
  82.4 1.3 %copy-start.7 = (bf16[8,1024]{1,0:T(8,128)(2,1)S(1)}, bf16[8,1024]{1,0:T(8,128)(2,1)}, u32[]{:S(2)}) copy-start(bf16[8,1024]{1,0:T(8,128)(2,1)} %get-tuple-element.35) | copy-start | bytes 49156

commit v2 on v0

v2 whole, which is shorter than its diff:
```python
import math

import jax
import jax.numpy as jnp
from jax import lax
from jax.experimental import pallas as pl
from jax.experimental.pallas import tpu as pltpu
from jax.sharding import PartitionSpec as P

QH = 32
KVH = 8
HD = 128
NPROMPT = 8
PLEN = 256
NGEN = 16
ROWS = 512
GROUP = QH // KVH
HEADS = 4
KV = 2
PLANE = 16
DEPTH = 4
CHUNK = 128
WIDE = GROUP * HD
SPAN = GROUP * CHUNK
CHUNKS = ROWS // CHUNK
MESH = pl.DeviceIdType.MESH
INV_SQRT = 1.0 / math.sqrt(HD)
EXP2_SCALE = INV_SQRT * math.log2(math.e)
NEG_FILL = -1e30
F32 = jnp.float32
BF16 = jnp.bfloat16


def place():
    seq = lax.axis_index("seq")
    head = lax.axis_index("head")
    return seq, head, seq // DEPTH, lax.rem(seq, DEPTH), seq // 8, 4 * lax.rem(seq, 8) + head


def spread_target(unit, i):
    return (unit // 2) * DEPTH + lax.rem(i, DEPTH), i // DEPTH


def holder_of(plane, i):
    unit = 2 * plane + lax.rem(i, 2)
    return 8 * (i // 2) + unit // 4, lax.rem(unit, 4)


def dot(a, b):
    return jnp.dot(a, b, preferred_element_type=F32)


def wait_bytes(ref, sem):
    pltpu.make_async_copy(ref, ref, sem).wait()


def kernel(
    owner_ref, comp_ref, q_hbm, k_hbm, v_hbm, pk_hbm, pv_hbm, g_hbm,
    out_hbm, qg_hbm, kg_hbm, vg_hbm, pkg_ref, pvg_ref,
    q_in, g_in, k_in, v_in, pk_in, pv_in,
    own_rows, dense, packed, picked, chosen_kv, info, infos, infos_smem,
    q_turn, g_turn, e_local, p_local, stats, w_prompt, d_prompt, w_local, d_local, o_turn, pair_turn,
    part, parts, pieces, finals, out_v, qg_v, kg_v, vg_v,
    in_sem, out_sem, local_sem, send_a, recv_a, send_i, recv_i, send_b, recv_b, send_c, recv_c, send_d, recv_d,
):
    seq, head, plane, z, slot, unit = place()
    barrier = pltpu.get_barrier_semaphore()

    def loop(lo, hi, body):
        def step(i, carry):
            body(i)
            return carry

        lax.fori_loop(lo, hi, step, 0)

    def peer(i):
        return lax.rem(plane + i, PLANE)

    def not_self(other, other_head):
        return jnp.logical_or(other != seq, other_head != head)

    def greet(i):
        for other, other_head in (spread_target(unit, i), holder_of(plane, i)):
            @pl.when(not_self(other, other_head))
            def _():
                pl.semaphore_signal(barrier, inc=1, device_id=(other, other_head), device_id_type=MESH)

    def greet_peer(i):
        pl.semaphore_signal(barrier, inc=1, device_id=(peer(i) * DEPTH + z, head), device_id_type=MESH)

    loop(0, 16, greet)
    loop(1, PLANE, greet_peer)

    loads = [
        pltpu.make_async_copy(pk_hbm, pk_in, in_sem.at[0]),
        pltpu.make_async_copy(pv_hbm, pv_in, in_sem.at[1]),
    ]
    for kv in range(KV):
        wide, narrow = pl.ds(kv * WIDE, WIDE), pl.ds(kv * HD, HD)
        for n, (src, dst, cols) in enumerate(
            ((q_hbm, q_in, wide), (k_hbm, k_in, narrow), (g_hbm, g_in, wide), (v_hbm, v_in, narrow))
        ):
            loads.append(pltpu.make_async_copy(src.at[:, cols], dst.at[kv], in_sem.at[2 + 4 * kv + n]))
    for load in loads:
        load.start()

    lead_comp = comp_ref[0]
    lead = owner_ref[lead_comp // NGEN]
    tail = owner_ref[comp_ref[ROWS - 1] // NGEN]
    split = jnp.int32(0)
    for step in (256, 128, 64, 32, 16, 8, 4, 2, 1):
        split = jnp.where(comp_ref[split + step - 1] == lead_comp, split + step, split)
    info[...] = jnp.where(lax.broadcasted_iota(jnp.int32, (8, 128), 0) < 4, lead, tail)
    infos[plane] = info[...]

    loads[0].wait()
    loads[1].wait()
    both = jnp.concatenate([pk_in[...].astype(F32), pv_in[...].astype(F32)], 0).astype(BF16)
    for other_head in range(HEADS):
        for kv in range(KV):
            lo = (KV * other_head + kv) * HD
            own_rows[other_head, kv] = both[:, lo : lo + HD]
    for load in loads[2:]:
        load.wait()

    lane_row = lax.broadcasted_iota(jnp.int32, (1, SPAN), 1) % CHUNK

    def before(kv):
        for chunk in range(CHUNKS):
            lo, hi = chunk * CHUNK, (chunk + 1) * CHUNK
            span = slice(chunk * SPAN, (chunk + 1) * SPAN)
            q_t = jnp.concatenate([q_in[kv, lo:hi, j * HD : (j + 1) * HD].T for j in range(GROUP)], 1)
            g_t = jnp.concatenate([g_in[kv, lo:hi, j * HD : (j + 1) * HD].T for j in range(GROUP)], 1)
            q_turn[kv, :, span] = q_t
            g_turn[kv, :, span] = g_t
            key_at = lax.broadcasted_iota(jnp.int32, (hi, CHUNK), 0)
            row_at = lo + lax.broadcasted_iota(jnp.int32, (hi, CHUNK), 1)
            seen = jnp.logical_and(key_at <= row_at, jnp.logical_or(key_at >= split, row_at < split))
            bias = jnp.where(seen, 0.0, NEG_FILL)
            scores = dot(k_in[kv, :hi], q_t) + jnp.concatenate([bias] * GROUP, 1)
            top = jnp.max(scores, axis=0, keepdims=True)
            raw = jnp.exp2((scores - top) * EXP2_SCALE)
            e_local[kv, :hi, span] = raw
            stats[kv, 0:1, span] = top
            stats[kv, 1:2, span] = jnp.sum(raw, axis=0, keepdims=True)
            p_local[kv, :hi, span] = dot(v_in[kv, :hi], g_t)

    def pair_of(turned, is_lead):
        zero = jnp.zeros_like(turned)
        return jnp.concatenate([jnp.where(is_lead, turned, zero), jnp.where(is_lead, zero, turned)], 0)

    def stacked(ref, kv):
        return jnp.concatenate(
            [
                ref[kv, c * CHUNK : (c + 1) * CHUNK, j * HD : (j + 1) * HD]
                for c in range(CHUNKS)
                for j in range(GROUP)
            ],
            0,
        )

    def stacked_pair(ref, kv):
        rows = stacked(ref, kv)
        at = lax.broadcasted_iota(jnp.int32, (GROUP * ROWS, 1), 0)
        in_lead = (at // SPAN) * CHUNK + at % CHUNK < split
        zero = jnp.zeros_like(rows)
        return jnp.concatenate([jnp.where(in_lead, rows, zero), jnp.where(in_lead, zero, rows)], 1)

    def middle(kv):
        key_pair = jnp.concatenate([chosen_kv[kv, :, t, 0].reshape(PLEN, HD) for t in range(2)], 1)
        value_pair = jnp.concatenate([chosen_kv[kv, :, t, 1].reshape(PLEN, HD) for t in range(2)], 1)
        pair_turn[kv] = key_pair.T
        value_pair_t = value_pair.T
        values_t = v_in[kv].T
        for chunk in range(CHUNKS):
            hi = (chunk + 1) * CHUNK
            span = slice(chunk * SPAN, (chunk + 1) * SPAN)
            is_lead = chunk * CHUNK + lane_row < split
            g_t = g_turn[kv, :, span]
            s_prompt = dot(key_pair, pair_of(q_turn[kv, :, span], is_lead))
            top_local = stats[kv, 0:1, span]
            top = jnp.maximum(top_local, jnp.max(s_prompt, axis=0, keepdims=True))
            e_prompt = jnp.exp2((s_prompt - top) * EXP2_SCALE)
            rescale = jnp.exp2((top_local - top) * EXP2_SCALE)
            inv = 1.0 / (jnp.sum(e_prompt, axis=0, keepdims=True) + rescale * stats[kv, 1:2, span])
            rescale = rescale * inv
            e_prompt = e_prompt * inv
            wh_prompt = e_prompt.astype(BF16)
            wh_local = (e_local[kv, :hi, span] * rescale).astype(BF16)
            w_prompt[kv, :, span] = wh_prompt
            w_local[kv, :hi, span] = wh_local
            o_pair = dot(value_pair_t, wh_prompt)
            o_t = jnp.where(is_lead, o_pair[:HD], o_pair[HD:]) + dot(values_t[:, :hi], wh_local)
            o_t = o_t.astype(BF16)
            o_turn[kv, :, span] = o_t
            delta = jnp.sum(o_t.astype(F32) * g_t.astype(F32), axis=0, keepdims=True)
            stats[kv, 2:3, span] = rescale
            stats[kv, 3:4, span] = delta
            d_prompt[kv, :, span] = (e_prompt * (dot(value_pair, pair_of(g_t, is_lead)) - delta)).astype(BF16)
        dk_pair = dot(d_prompt[kv], stacked_pair(q_in, kv)) * INV_SQRT
        dv_pair = dot(w_prompt[kv], stacked_pair(g_in, kv))
        for t in range(2):
            part[kv, :, t, 0] = dk_pair[:, t * HD : (t + 1) * HD].astype(BF16).reshape(PLANE, 16, HD)
            part[kv, :, t, 1] = dv_pair[:, t * HD : (t + 1) * HD].astype(BF16).reshape(PLANE, 16, HD)

    def after(kv):
        keys_t = k_in[kv].T
        for chunk in range(CHUNKS):
            lo, hi = chunk * CHUNK, (chunk + 1) * CHUNK
            span = slice(chunk * SPAN, (chunk + 1) * SPAN)
            is_lead = lo + lane_row < split
            rescale = stats[kv, 2:3, span]
            delta = stats[kv, 3:4, span]
            ds_local = ((e_local[kv, :hi, span] * rescale) * (p_local[kv, :hi, span] - delta)).astype(BF16)
            d_local[kv, :hi, span] = ds_local
            dq_pair = dot(pair_turn[kv], d_prompt[kv, :, span])
            dq_t = jnp.where(is_lead, dq_pair[:HD], dq_pair[HD:]) + dot(keys_t[:, :hi], ds_local)
            dq_t = (dq_t * INV_SQRT).astype(BF16)
            o_t = o_turn[kv, :, span]
            for j in range(GROUP):
                cols = slice(j * HD, (j + 1) * HD)
                out_v[kv, lo:hi, cols] = o_t[:, j * CHUNK : (j + 1) * CHUNK].T
                qg_v[kv, lo:hi, cols] = dq_t[:, j * CHUNK : (j + 1) * CHUNK].T
        q_all = stacked(q_in, kv)
        g_all = stacked(g_in, kv)
        for chunk in range(CHUNKS):
            lo, hi = chunk * CHUNK, (chunk + 1) * CHUNK
            start = chunk * SPAN
            kg_v[kv, lo:hi] = (dot(d_local[kv, lo:hi, start:], q_all[start:]) * INV_SQRT).astype(BF16)
            vg_v[kv, lo:hi] = dot(w_local[kv, lo:hi, start:], g_all[start:]).astype(BF16)

    def store(kv, n, src, dst, width):
        cols = pl.ds(pl.multiple_of(kv * width, width), width)
        return pltpu.make_async_copy(src.at[kv], dst.at[:, cols], out_sem.at[4 * kv + n])

    def stores(kv):
        return (
            store(kv, 0, out_v, out_hbm, WIDE), store(kv, 1, qg_v, qg_hbm, WIDE),
            store(kv, 2, kg_v, kg_hbm, HD), store(kv, 3, vg_v, vg_hbm, HD),
        )

    def copy_a(i):
        other, other_head = spread_target(unit, i)
        at = 2 * slot + lax.rem(unit, 2)
        return not_self(other, other_head), pltpu.make_async_remote_copy(
            src_ref=own_rows.at[i // DEPTH], dst_ref=dense.at[at], send_sem=send_a.at[i], recv_sem=recv_a.at[at],
            device_id=(other, other_head), device_id_type=MESH,
        )

    def start_a(i):
        away, copy = copy_a(i)

        @pl.when(jnp.logical_not(away))
        def _():
            at = 2 * slot + lax.rem(unit, 2)
            pltpu.make_async_copy(own_rows.at[i // DEPTH], dense.at[at], recv_a.at[at]).start()

        @pl.when(away)
        def _():
            copy.start()

    def copy_info(i):
        return pltpu.make_async_remote_copy(
            src_ref=info, dst_ref=infos.at[plane], send_sem=send_i.at[i], recv_sem=recv_i.at[plane],
            device_id=(peer(i) * DEPTH + z, head), device_id_type=MESH,
        )

    def copy_b(kv, i):
        return pltpu.make_async_remote_copy(
            src_ref=picked.at[kv, i], dst_ref=chosen_kv.at[kv, plane],
            send_sem=send_b.at[kv, i], recv_sem=recv_b.at[kv, plane],
            device_id=(peer(i) * DEPTH + z, head), device_id_type=MESH,
        )

    def copy_c(kv, i):
        return pltpu.make_async_remote_copy(
            src_ref=part.at[kv, peer(i)], dst_ref=parts.at[kv, plane],
            send_sem=send_c.at[kv, i], recv_sem=recv_c.at[kv, plane],
            device_id=(peer(i) * DEPTH + z, head), device_id_type=MESH,
        )

    def copy_d(i):
        other, other_head = holder_of(plane, i)
        at = DEPTH * head + z
        return not_self(other, other_head), pltpu.make_async_remote_copy(
            src_ref=pieces.at[i], dst_ref=finals.at[at], send_sem=send_d.at[i], recv_sem=recv_d.at[at],
            device_id=(other, other_head), device_id_type=MESH,
        )

    def start_d(i):
        away, copy = copy_d(i)

        @pl.when(jnp.logical_not(away))
        def _():
            at = DEPTH * head + z
            pltpu.make_async_copy(pieces.at[i], finals.at[at], recv_d.at[at]).start()

        @pl.when(away)
        def _():
            copy.start()

    before(0)
    own = unit // 2 == plane

    @pl.when(own)
    def _():
        pl.semaphore_wait(barrier, 15 + 30)

    @pl.when(jnp.logical_not(own))
    def _():
        pl.semaphore_wait(barrier, 15 + 32)

    loop(0, 16, start_a)
    loop(1, PLANE, lambda i: copy_info(i).start())
    before(1)
    loop(1, PLANE, lambda i: wait_bytes(infos.at[peer(i)], recv_i.at[peer(i)]))
    to_smem = pltpu.make_async_copy(infos, infos_smem, local_sem)
    to_smem.start()
    loop(0, 16, lambda i: wait_bytes(dense.at[i], recv_a.at[i]))
    to_smem.wait()
    for p in range(NPROMPT):
        for kv in range(KV):
            first = dense[2 * p, kv].astype(F32)
            second = dense[2 * p + 1, kv].astype(F32)
            packed[kv, p, 0] = jnp.concatenate([first[:8], second[:8]], 0).astype(BF16)
            packed[kv, p, 1] = jnp.concatenate([first[8:], second[8:]], 0).astype(BF16)

    for kv in range(KV):
        def start_b(i):
            picked[kv, i, 0] = packed[kv, infos_smem[peer(i), 0, 0]]
            picked[kv, i, 1] = packed[kv, infos_smem[peer(i), 4, 0]]
            copy_b(kv, i).start()

        loop(1, PLANE, start_b)
        chosen_kv[kv, plane, 0] = packed[kv, lead]
        chosen_kv[kv, plane, 1] = packed[kv, tail]

    def middle_step(kv):
        loop(1, PLANE, lambda i: wait_bytes(chosen_kv.at[kv, peer(i)], recv_b.at[kv, peer(i)]))
        middle(kv)
        loop(1, PLANE, lambda i: copy_c(kv, i).start())
        parts[kv, plane] = part[kv, plane]

    loop(0, KV, middle_step)

    terms = 2 * PLANE * 16
    lane = lax.broadcasted_iota(jnp.int32, (1, terms), 1)
    lane_slot = jnp.zeros((1, terms), jnp.int32)
    for i in range(PLANE):
        lane_slot = jnp.where(lane // 16 == 2 * i, infos_smem[i, 0, 0], lane_slot)
        lane_slot = jnp.where(lane // 16 == 2 * i + 1, infos_smem[i, 4, 0], lane_slot)
    row = lax.broadcasted_iota(jnp.int32, (NPROMPT * 16, terms), 0)
    lanes = lax.broadcasted_iota(jnp.int32, (NPROMPT * 16, terms), 1)
    chosen = jnp.logical_and(row // 16 == lane_slot, lax.rem(row, 16) == lax.rem(lanes, 16))
    chosen = jnp.where(chosen, 1.0, 0.0).astype(BF16)

    def after_step(kv):
        after(kv)
        for copy in stores(kv):
            copy.start()

    loop(0, KV, after_step)

    for kv in range(KV):
        loop(1, PLANE, lambda i: wait_bytes(parts.at[kv, peer(i)], recv_c.at[kv, peer(i)]))
        sums = [dot(chosen, parts[kv, :, :, n].reshape(terms, HD)) for n in range(2)]
        for i in range(2 * NPROMPT):
            lo = 8 * i
            pieces[i, kv] = jnp.concatenate([sums[0][lo : lo + 8], sums[1][lo : lo + 8]], 0).astype(BF16)
    loop(0, 16, start_d)

    def wait_sends(i):
        copy_info(i).wait_send()
        for kv in range(KV):
            copy_b(kv, i).wait_send()
            copy_c(kv, i).wait_send()

    def wait_send_a(i):
        away, copy = copy_a(i)

        @pl.when(away)
        def _():
            copy.wait_send()

    def wait_send_d(i):
        away, copy = copy_d(i)

        @pl.when(away)
        def _():
            copy.wait_send()

    loop(1, PLANE, wait_sends)
    loop(0, 16, wait_send_a)
    for kv in range(KV):
        for copy in stores(kv):
            copy.wait()
    loop(0, 16, lambda i: wait_bytes(finals.at[i], recv_d.at[i]))
    for other_head in range(HEADS):
        for kv in range(KV):
            total = finals[DEPTH * other_head, kv].astype(F32)
            for other_z in range(1, DEPTH):
                total = total + finals[DEPTH * other_head + other_z, kv].astype(F32)
            lo = (KV * other_head + kv) * HD
            pkg_ref[:, lo : lo + HD] = total[:8].astype(BF16)
            pvg_ref[:, lo : lo + HD] = total[8:].astype(BF16)
    loop(0, 16, wait_send_d)


def shards(query, comp_key, comp_value, prompt_key, prompt_value, out_grad, row_comp, prompt_owner):
    vmem = pl.BlockSpec(memory_space=pltpu.VMEM)
    smem = pl.BlockSpec(memory_space=pltpu.SMEM)
    hbm = pl.BlockSpec(memory_space=pl.ANY)
    dma = pltpu.SemaphoreType.DMA
    wide_rows = (KV, ROWS, WIDE)
    rows = (KV, ROWS, HD)
    heads_wide = GROUP * ROWS
    prompt_rows = prompt_key.shape
    like = lambda a: jax.ShapeDtypeStruct(a.shape, BF16)
    buf = pltpu.VMEM
    return pl.pallas_call(
        kernel,
        out_shape=(
            like(query), like(query), like(comp_key), like(comp_value), like(prompt_key), like(prompt_value),
        ),
        in_specs=[smem, smem] + [hbm] * 6,
        out_specs=(hbm, hbm, hbm, hbm, vmem, vmem),
        scratch_shapes=[
            buf(wide_rows, BF16), buf(wide_rows, BF16), buf(rows, BF16), buf(rows, BF16),
            buf(prompt_rows, BF16), buf(prompt_rows, BF16),
            buf((HEADS, KV, 16, HD), BF16),
            buf((16, KV, 16, HD), BF16),
            buf((KV, NPROMPT, 2, 16, HD), BF16),
            buf((KV, PLANE, 2, 2, 16, HD), BF16),
            buf((KV, PLANE, 2, 2, 16, HD), BF16),
            buf((8, 128), jnp.int32),
            buf((PLANE, 8, 128), jnp.int32),
            pltpu.SMEM((PLANE, 8, 128), jnp.int32),
            buf((KV, HD, heads_wide), BF16),
            buf((KV, HD, heads_wide), BF16),
            buf((KV, ROWS, heads_wide), F32),
            buf((KV, ROWS, heads_wide), F32),
            buf((KV, 8, heads_wide), F32),
            buf((KV, PLEN, heads_wide), BF16),
            buf((KV, PLEN, heads_wide), BF16),
            buf((KV, ROWS, heads_wide), BF16),
            buf((KV, ROWS, heads_wide), BF16),
            buf((KV, HD, heads_wide), BF16),
            buf((KV, 2 * HD, PLEN), BF16),
            buf((KV, PLANE, 2, 2, 16, HD), BF16),
            buf((KV, PLANE, 2, 2, 16, HD), BF16),
            buf((16, KV, 16, HD), BF16),
            buf((16, KV, 16, HD), BF16),
            buf(wide_rows, BF16), buf(wide_rows, BF16), buf(rows, BF16), buf(rows, BF16),
            dma((10,)), dma((8,)), dma,
            dma((16,)), dma((16,)), dma((PLANE,)), dma((PLANE,)),
            dma((KV, PLANE)), dma((KV, PLANE)), dma((KV, PLANE)), dma((KV, PLANE)),
            dma((16,)), dma((16,)),
        ],
        compiler_params=pltpu.CompilerParams(
            collective_id=0, has_side_effects=True, vmem_limit_bytes=56 * 1024 * 1024
        ),
        name="attend",
    )(prompt_owner, row_comp, query, comp_key, comp_value, prompt_key, prompt_value, out_grad)


def solution(mesh):
    placed = (
        P("seq", "head"),
        P("seq", "head"),
        P("seq", "head"),
        P(("seq", "head"), None),
        P(("seq", "head"), None),
        P("seq", "head"),
        P("seq"),
        P(),
    )
    return jax.shard_map(
        shards,
        mesh=mesh,
        in_specs=placed,
        out_specs=(
            P("seq", "head"),
            P("seq", "head"),
            P("seq", "head"),
            P("seq", "head"),
            P(("seq", "head"), None),
            P(("seq", "head"), None),
        ),
        check_vma=False,
    )
```

time: 708 us -> 62.4 us (0.09)
  the two profiles are of different devices: /device:TPU:1 before, /device:TPU:25 now
where the time goes in v2:
time: 62.4 us; the launch traced here: 62 us
  Pallas kernels  54.8 us (88%)
  local copies, waits for them, and re-layouts  6.53 us (10%)
  between operations  0.66 us (1%)
    pallas_call x1, Pallas kernels, shards(): pl.pallas_call(kernel, out_shape=(like(query), like(query), like(comp_key...  54.8 us
    unnamed x16, local copies, waits for them, and re-layouts  6.53 us

profile of v2, /device:TPU:25, one launch (start us, length us, event | category | flops | bytes accessed | tf_op | source)
XLA Modules:
  0.0 62.0 jit_solution(16057757825504117151)
XLA Ops:
  0.6 54.8 %attend.1 = (bf16[512,1024]{1,0:T(8,128)(2,1)}, bf16[512,1024]{1,0:T(8,128)(2,1)}, bf16[512,256]{1,0:T(8,128)(2,1)}, bf16[512,256]{1,0:T(8,128)(2,1)}, bf16[8,1024]{1,0:T(8,128)(2,1)}, /*index=5*/bf16[8,1024]{1,0:T(8,128)(2,1)}) custom-call(s32[8]{0:T(128)} %owner_ref.1, s32[512]{0:T(512)} %comp_ref.1, bf16[512,1024]{1,0:T(8,128)(2,1)} %q_hbm.1, ...), custom_call_target="tpu_custom_call" | custom-call | tf_op jit(solution)/shard_map/attend/pallas_call | solution.py:420
  55.4 0.0 copy-start
  55.4 2.4 %copy.20 = bf16[512,1024]{1,0:T(8,128)(2,1)} copy(bf16[512,1024]{1,0:T(8,128)(2,1)} %get-tuple-element.12) | data formatting | bytes 2097152
  57.8 0.0 copy-done
  57.8 0.0 copy-start.2
  57.8 1.0 %copy.21 = bf16[512,1024]{1,0:T(8,128)(2,1)} copy(bf16[512,1024]{1,0:T(8,128)(2,1)S(1)} %copy-done) | data formatting | bytes 2097152
  58.8 0.1 copy-done.2
  58.9 0.0 copy-start.1
  58.9 0.7 %copy.22 = bf16[512,256]{1,0:T(8,128)(2,1)} copy(bf16[512,256]{1,0:T(8,128)(2,1)S(1)} %copy-done.2) | data formatting | bytes 524288
  59.6 0.3 copy-done.1
  59.9 0.0 copy-start.4
  59.9 0.7 %copy.23 = bf16[512,256]{1,0:T(8,128)(2,1)} copy(bf16[512,256]{1,0:T(8,128)(2,1)S(1)} %copy-done.1) | data formatting | bytes 524288
  60.6 0.0 copy-done.4
  60.7 0.0 copy-start.3
  60.7 0.6 copy.24
  61.3 0.1 copy-done.3
  61.4 0.6 copy.25
Async XLA Ops:
  55.4 2.4 %copy-start = (bf16[512,1024]{1,0:T(8,128)(2,1)S(1)}, bf16[512,1024]{1,0:T(8,128)(2,1)}, u32[]{:S(2)}) copy-start(bf16[512,1024]{1,0:T(8,128)(2,1)} %get-tuple-element.13) | copy-start | bytes 3145732
  57.8 1.1 %copy-start.2 = (bf16[512,256]{1,0:T(8,128)(2,1)S(1)}, bf16[512,256]{1,0:T(8,128)(2,1)}, u32[]{:S(2)}) copy-start(bf16[512,256]{1,0:T(8,128)(2,1)} %get-tuple-element.14) | copy-start | bytes 786436
  58.9 1.0 %copy-start.1 = (bf16[512,256]{1,0:T(8,128)(2,1)S(1)}, bf16[512,256]{1,0:T(8,128)(2,1)}, u32[]{:S(2)}) copy-start(bf16[512,256]{1,0:T(8,128)(2,1)} %get-tuple-element.15) | copy-start | bytes 786436
  59.9 0.7 %copy-start.4 = (bf16[8,1024]{1,0:T(8,128)(2,1)S(1)}, bf16[8,1024]{1,0:T(8,128)(2,1)}, u32[]{:S(2)}) copy-start(bf16[8,1024]{1,0:T(8,128)(2,1)} %get-tuple-element.16) | copy-start | bytes 49156
  60.7 0.7 %copy-start.3 = (bf16[8,1024]{1,0:T(8,128)(2,1)S(1)}, bf16[8,1024]{1,0:T(8,128)(2,1)}, u32[]{:S(2)}) copy-start(bf16[8,1024]{1,0:T(8,128)(2,1)} %get-tuple-element.17) | copy-start | bytes 49156

commit v3 on v2

v3 whole, which is shorter than its diff:
```python
import math

import jax
import jax.numpy as jnp
from jax import lax
from jax.experimental import pallas as pl
from jax.experimental.pallas import tpu as pltpu
from jax.sharding import PartitionSpec as P

QH = 32
KVH = 8
HD = 128
NPROMPT = 8
PLEN = 256
NGEN = 16
ROWS = 512
GROUP = QH // KVH
HEADS = 4
KV = 2
PLANE = 16
DEPTH = 4
CHUNK = 128
WIDE = GROUP * HD
SPAN = GROUP * CHUNK
CHUNKS = ROWS // CHUNK
MESH = pl.DeviceIdType.MESH
INV_SQRT = 1.0 / math.sqrt(HD)
EXP2_SCALE = INV_SQRT * math.log2(math.e)
NEG_FILL = -1e30
F32 = jnp.float32
BF16 = jnp.bfloat16


def place():
    seq = lax.axis_index("seq")
    head = lax.axis_index("head")
    x, y, z = seq // 16, lax.rem(seq // 4, 4), lax.rem(seq, 4)
    return seq, head, x, y, z, 2 * z + head // 2, lax.rem(head, 2), seq // 8


FAR_Z = (2, 1, 3, 0)
FAR_Z8 = (4, 3, 5, 2, 6, 1, 7, 0)
FAR_XY = sorted(
    ((dx, dy) for dx in range(4) for dy in range(4) if (dx, dy) != (0, 0)),
    key=lambda d: -(min(d[0], 4 - d[0]) + min(d[1], 4 - d[1])),
)


def dot(a, b):
    return jnp.dot(a, b, preferred_element_type=F32)


def wait_bytes(ref, sem):
    pltpu.make_async_copy(ref, ref, sem).wait()


def kernel(
    owner_hbm, comp_hbm, q_hbm, k_hbm, v_hbm, pk_hbm, pv_hbm, g_hbm,
    out_hbm, qg_hbm, kg_hbm, vg_hbm, pkg_ref, pvg_ref,
    owner_ref, comp_ref, q_in, g_in, k_in, v_in, pk_in, pv_in,
    own_rows, dense, packed, picked, chosen_kv, info, infos, infos_smem,
    q_turn, g_turn, e_local, p_local, o_local, stats, w_prompt, d_prompt, w_local, d_local, o_turn, pair_turn,
    part, parts, pieces, finals, out_v, qg_v, kg_v, vg_v,
    in_sem, out_sem, local_sem, send_a, recv_a, send_i, recv_i, send_b, recv_b, send_c, recv_c, send_d, recv_d,
):
    seq, head, x, y, z, z8, core, slot = place()
    plane = 4 * x + y
    barrier = pltpu.get_barrier_semaphore()

    served = lax.rem(z8 - slot + 8, 8)
    column = 4 * (served // 2) + 2 * lax.rem(served, 2) + lax.rem(y, 2)
    own = column == plane
    self_slot = lax.rem(z8 - slot + 8, 8) == slot

    def spread_target(dz, other_head):
        return column * DEPTH + lax.rem(z + dz, DEPTH), jnp.int32(other_head)

    def holder(off, k):
        other_slot = lax.rem(z8 + off - slot + 8, 8)
        other_z8 = lax.rem(z8 + off, 8)
        other_y = 2 * lax.rem(other_slot, 2) + lax.rem(y, 2)
        other = 16 * (other_slot // 2) + 4 * other_y + other_z8 // 2
        return other_slot, other, 2 * lax.rem(other_z8, 2) + k

    def xy_peer(d):
        return 4 * lax.rem(x + d[0], 4) + lax.rem(y + d[1], 4)

    def signal(other, other_head):
        pl.semaphore_signal(barrier, inc=1, device_id=(other, other_head), device_id_type=MESH)

    def greet_spread(dz):
        for other_head in range(HEADS):
            other, _ = spread_target(dz, other_head)
            if dz:
                signal(other, jnp.int32(other_head))
            else:
                @pl.when(jnp.logical_not(jnp.logical_and(own, head == other_head)))
                def _():
                    signal(other, jnp.int32(other_head))

    def greet_holder(off):
        for k in range(2):
            _, other, other_head = holder(off, k)
            if off:
                signal(other, other_head)
            else:
                @pl.when(jnp.logical_not(jnp.logical_and(self_slot, core == k)))
                def _():
                    signal(other, other_head)

    greet_spread(2)
    for off in (4, 3, 5):
        greet_holder(off)
    greet_spread(1)
    greet_spread(3)
    for off in (2, 6):
        greet_holder(off)
    greet_spread(0)
    for off in (1, 7, 0):
        greet_holder(off)
    for d in FAR_XY:
        signal(xy_peer(d) * DEPTH + z, head)

    loads = [
        pltpu.make_async_copy(pk_hbm, pk_in, in_sem.at[0]),
        pltpu.make_async_copy(pv_hbm, pv_in, in_sem.at[1]),
        pltpu.make_async_copy(owner_hbm, owner_ref, in_sem.at[10]),
        pltpu.make_async_copy(comp_hbm, comp_ref, in_sem.at[11]),
    ]
    for kv in range(KV):
        wide, narrow = pl.ds(kv * WIDE, WIDE), pl.ds(kv * HD, HD)
        for n, (src, dst, cols) in enumerate(
            ((q_hbm, q_in, wide), (k_hbm, k_in, narrow), (g_hbm, g_in, wide), (v_hbm, v_in, narrow))
        ):
            loads.append(pltpu.make_async_copy(src.at[:, cols], dst.at[kv], in_sem.at[2 + 4 * kv + n]))
    for load in loads:
        load.start()
    for load in loads[:4]:
        load.wait()

    both = jnp.concatenate([pk_in[...].astype(F32), pv_in[...].astype(F32)], 0).astype(BF16)
    for other_head in range(HEADS):
        for kv in range(KV):
            lo = (KV * other_head + kv) * HD
            own_rows[other_head, kv] = both[:, lo : lo + HD]

    lead_comp = comp_ref[0]
    lead = owner_ref[lead_comp // NGEN]
    tail = owner_ref[comp_ref[ROWS - 1] // NGEN]
    split = jnp.int32(0)
    for step in (256, 128, 64, 32, 16, 8, 4, 2, 1):
        split = jnp.where(comp_ref[split + step - 1] == lead_comp, split + step, split)
    info[...] = jnp.where(lax.broadcasted_iota(jnp.int32, (8, 128), 0) < 4, lead, tail)
    infos[plane] = info[...]

    for load in loads[4:]:
        load.wait()

    def loop(lo, hi, body):
        def step(i, carry):
            body(i)
            return carry

        lax.fori_loop(lo, hi, step, 0)

    lane_row = lax.broadcasted_iota(jnp.int32, (1, SPAN), 1) % CHUNK

    def before(kv):
        values_t = v_in[kv].T
        for chunk in range(CHUNKS):
            lo, hi = chunk * CHUNK, (chunk + 1) * CHUNK
            span = slice(chunk * SPAN, (chunk + 1) * SPAN)
            q_t = jnp.concatenate([q_in[kv, lo:hi, j * HD : (j + 1) * HD].T for j in range(GROUP)], 1)
            g_t = jnp.concatenate([g_in[kv, lo:hi, j * HD : (j + 1) * HD].T for j in range(GROUP)], 1)
            q_turn[kv, :, span] = q_t
            g_turn[kv, :, span] = g_t
            key_at = lax.broadcasted_iota(jnp.int32, (hi, CHUNK), 0)
            row_at = lo + lax.broadcasted_iota(jnp.int32, (hi, CHUNK), 1)
            seen = jnp.logical_and(key_at <= row_at, jnp.logical_or(key_at >= split, row_at < split))
            bias = jnp.where(seen, 0.0, NEG_FILL)
            scores = dot(k_in[kv, :hi], q_t) + jnp.concatenate([bias] * GROUP, 1)
            top = jnp.max(scores, axis=0, keepdims=True)
            raw = jnp.exp2((scores - top) * EXP2_SCALE)
            e_local[kv, :hi, span] = raw
            o_local[kv, :, span] = dot(values_t[:, :hi], raw.astype(BF16))
            stats[kv, 0:1, span] = top
            stats[kv, 1:2, span] = jnp.sum(raw, axis=0, keepdims=True)
            p_local[kv, :hi, span] = dot(v_in[kv, :hi], g_t)

    def pair_of(turned, is_lead):
        zero = jnp.zeros_like(turned)
        return jnp.concatenate([jnp.where(is_lead, turned, zero), jnp.where(is_lead, zero, turned)], 0)

    def stacked(ref, kv):
        return jnp.concatenate(
            [
                ref[kv, c * CHUNK : (c + 1) * CHUNK, j * HD : (j + 1) * HD]
                for c in range(CHUNKS)
                for j in range(GROUP)
            ],
            0,
        )

    def stacked_pair(ref, kv):
        rows = stacked(ref, kv)
        at = lax.broadcasted_iota(jnp.int32, (GROUP * ROWS, 1), 0)
        in_lead = (at // SPAN) * CHUNK + at % CHUNK < split
        zero = jnp.zeros_like(rows)
        return jnp.concatenate([jnp.where(in_lead, rows, zero), jnp.where(in_lead, zero, rows)], 1)

    def middle(kv):
        key_pair = jnp.concatenate([chosen_kv[:, kv, t, 0].reshape(PLEN, HD) for t in range(2)], 1)
        value_pair = jnp.concatenate([chosen_kv[:, kv, t, 1].reshape(PLEN, HD) for t in range(2)], 1)
        pair_turn[kv] = key_pair.T
        value_pair_t = value_pair.T
        for chunk in range(CHUNKS):
            span = slice(chunk * SPAN, (chunk + 1) * SPAN)
            is_lead = chunk * CHUNK + lane_row < split
            g_t = g_turn[kv, :, span]
            s_prompt = dot(key_pair, pair_of(q_turn[kv, :, span], is_lead))
            top_local = stats[kv, 0:1, span]
            top = jnp.maximum(top_local, jnp.max(s_prompt, axis=0, keepdims=True))
            e_prompt = jnp.exp2((s_prompt - top) * EXP2_SCALE)
            rescale = jnp.exp2((top_local - top) * EXP2_SCALE)
            inv = 1.0 / (jnp.sum(e_prompt, axis=0, keepdims=True) + rescale * stats[kv, 1:2, span])
            rescale = rescale * inv
            e_prompt = e_prompt * inv
            wh_prompt = e_prompt.astype(BF16)
            w_prompt[kv, :, span] = wh_prompt
            o_pair = dot(value_pair_t, wh_prompt)
            o_t = jnp.where(is_lead, o_pair[:HD], o_pair[HD:]) + o_local[kv, :, span] * rescale
            o_t = o_t.astype(BF16)
            o_turn[kv, :, span] = o_t
            delta = jnp.sum(o_t.astype(F32) * g_t.astype(F32), axis=0, keepdims=True)
            stats[kv, 2:3, span] = rescale
            stats[kv, 3:4, span] = delta
            d_prompt[kv, :, span] = (e_prompt * (dot(value_pair, pair_of(g_t, is_lead)) - delta)).astype(BF16)
        dk_pair = dot(d_prompt[kv], stacked_pair(q_in, kv)) * INV_SQRT
        dv_pair = dot(w_prompt[kv], stacked_pair(g_in, kv))
        for t in range(2):
            part[kv, :, t, 0] = dk_pair[:, t * HD : (t + 1) * HD].astype(BF16).reshape(PLANE, 16, HD)
            part[kv, :, t, 1] = dv_pair[:, t * HD : (t + 1) * HD].astype(BF16).reshape(PLANE, 16, HD)

    def after(kv):
        keys_t = k_in[kv].T
        for chunk in range(CHUNKS):
            lo, hi = chunk * CHUNK, (chunk + 1) * CHUNK
            span = slice(chunk * SPAN, (chunk + 1) * SPAN)
            is_lead = lo + lane_row < split
            rescale = stats[kv, 2:3, span]
            delta = stats[kv, 3:4, span]
            weights = e_local[kv, :hi, span] * rescale
            w_local[kv, :hi, span] = weights.astype(BF16)
            ds_local = (weights * (p_local[kv, :hi, span] - delta)).astype(BF16)
            d_local[kv, :hi, span] = ds_local
            dq_pair = dot(pair_turn[kv], d_prompt[kv, :, span])
            dq_t = jnp.where(is_lead, dq_pair[:HD], dq_pair[HD:]) + dot(keys_t[:, :hi], ds_local)
            dq_t = (dq_t * INV_SQRT).astype(BF16)
            o_t = o_turn[kv, :, span]
            for j in range(GROUP):
                cols = slice(j * HD, (j + 1) * HD)
                out_v[kv, lo:hi, cols] = o_t[:, j * CHUNK : (j + 1) * CHUNK].T
                qg_v[kv, lo:hi, cols] = dq_t[:, j * CHUNK : (j + 1) * CHUNK].T
        q_all = stacked(q_in, kv)
        g_all = stacked(g_in, kv)
        for chunk in range(CHUNKS):
            lo, hi = chunk * CHUNK, (chunk + 1) * CHUNK
            start = chunk * SPAN
            kg_v[kv, lo:hi] = (dot(d_local[kv, lo:hi, start:], q_all[start:]) * INV_SQRT).astype(BF16)
            vg_v[kv, lo:hi] = dot(w_local[kv, lo:hi, start:], g_all[start:]).astype(BF16)

    def store(kv, n, src, dst, width):
        cols = pl.ds(pl.multiple_of(kv * width, width), width)
        return pltpu.make_async_copy(src.at[kv], dst.at[:, cols], out_sem.at[4 * kv + n])

    def stores(kv):
        return (
            store(kv, 0, out_v, out_hbm, WIDE), store(kv, 1, qg_v, qg_hbm, WIDE),
            store(kv, 2, kg_v, kg_hbm, HD), store(kv, 3, vg_v, vg_hbm, HD),
        )

    def copy_a(dz, other_head):
        at = 2 * slot + core
        return pltpu.make_async_remote_copy(
            src_ref=own_rows.at[other_head], dst_ref=dense.at[at],
            send_sem=send_a.at[4 * dz + other_head], recv_sem=recv_a.at[at],
            device_id=spread_target(dz, other_head), device_id_type=MESH,
        )

    def self_a(other_head):
        return jnp.logical_and(own, head == other_head)

    def start_a(dz, other_head):
        if dz:
            copy_a(dz, other_head).start()
            return
        at = 2 * slot + core

        @pl.when(self_a(other_head))
        def _():
            pltpu.make_async_copy(own_rows.at[other_head], dense.at[at], recv_a.at[at]).start()

        @pl.when(jnp.logical_not(self_a(other_head)))
        def _():
            copy_a(dz, other_head).start()

    def wait_send_a(dz, other_head):
        if dz:
            copy_a(dz, other_head).wait_send()
            return

        @pl.when(jnp.logical_not(self_a(other_head)))
        def _():
            copy_a(dz, other_head).wait_send()

    def copy_info(n):
        return pltpu.make_async_remote_copy(
            src_ref=info, dst_ref=infos.at[plane], send_sem=send_i.at[n], recv_sem=recv_i.at[plane],
            device_id=(xy_peer(FAR_XY[n]) * DEPTH + z, head), device_id_type=MESH,
        )

    def copy_b(n):
        return pltpu.make_async_remote_copy(
            src_ref=picked.at[n], dst_ref=chosen_kv.at[plane], send_sem=send_b.at[n], recv_sem=recv_b.at[plane],
            device_id=(xy_peer(FAR_XY[n]) * DEPTH + z, head), device_id_type=MESH,
        )

    def copy_c(kv, n):
        other = xy_peer(FAR_XY[n])
        return pltpu.make_async_remote_copy(
            src_ref=part.at[kv, other], dst_ref=parts.at[kv, plane],
            send_sem=send_c.at[kv, n], recv_sem=recv_c.at[kv, plane],
            device_id=(other * DEPTH + z, head), device_id_type=MESH,
        )

    def copy_d(off, k):
        other_slot, other, other_head = holder(off, k)
        at = DEPTH * head + z
        return other_slot, pltpu.make_async_remote_copy(
            src_ref=pieces.at[2 * other_slot + k], dst_ref=finals.at[at],
            send_sem=send_d.at[2 * off + k], recv_sem=recv_d.at[at],
            device_id=(other, other_head), device_id_type=MESH,
        )

    def self_d(k):
        return jnp.logical_and(self_slot, core == k)

    def start_d(off, k):
        other_slot, copy = copy_d(off, k)
        if off:
            copy.start()
            return
        at = DEPTH * head + z

        @pl.when(self_d(k))
        def _():
            pltpu.make_async_copy(pieces.at[2 * other_slot + k], finals.at[at], recv_d.at[at]).start()

        @pl.when(jnp.logical_not(self_d(k)))
        def _():
            copy.start()

    def wait_send_d(off, k):
        _, copy = copy_d(off, k)
        if off:
            copy.wait_send()
            return

        @pl.when(jnp.logical_not(self_d(k)))
        def _():
            copy.wait_send()

    before(0)

    @pl.when(own)
    def _():
        pl.semaphore_wait(barrier, 15 + 15 + 15)

    @pl.when(jnp.logical_not(own))
    def _():
        pl.semaphore_wait(barrier, 15 + 16 + 16)

    for dz in FAR_Z:
        for other_head in range(HEADS):
            start_a(dz, other_head)
    for n in range(PLANE - 1):
        copy_info(n).start()
    before(1)
    for d in FAR_XY:
        other = xy_peer(d)
        wait_bytes(infos.at[other], recv_i.at[other])
    to_smem = pltpu.make_async_copy(infos, infos_smem, local_sem)
    to_smem.start()
    loop(0, 16, lambda i: wait_bytes(dense.at[i], recv_a.at[i]))
    to_smem.wait()
    for p in range(NPROMPT):
        for kv in range(KV):
            first = dense[2 * p, kv].astype(F32)
            second = dense[2 * p + 1, kv].astype(F32)
            packed[p, kv, 0] = jnp.concatenate([first[:8], second[:8]], 0).astype(BF16)
            packed[p, kv, 1] = jnp.concatenate([first[8:], second[8:]], 0).astype(BF16)
    for n, d in enumerate(FAR_XY):
        other = xy_peer(d)
        other_lead = infos_smem[other, 0, 0]
        other_tail = infos_smem[other, 4, 0]
        for kv in range(KV):
            picked[n, kv, 0] = packed[other_lead, kv]
            picked[n, kv, 1] = packed[other_tail, kv]
        copy_b(n).start()
    for kv in range(KV):
        chosen_kv[plane, kv, 0] = packed[lead, kv]
        chosen_kv[plane, kv, 1] = packed[tail, kv]
    for d in FAR_XY:
        other = xy_peer(d)
        wait_bytes(chosen_kv.at[other], recv_b.at[other])

    def middle_step(kv):
        middle(kv)
        for n in range(PLANE - 1):
            copy_c(kv, n).start()
        parts[kv, plane] = part[kv, plane]

    loop(0, KV, middle_step)

    terms = 2 * PLANE * 16
    lane = lax.broadcasted_iota(jnp.int32, (1, terms), 1)
    lane_slot = jnp.zeros((1, terms), jnp.int32)
    for i in range(PLANE):
        lane_slot = jnp.where(lane // 16 == 2 * i, infos_smem[i, 0, 0], lane_slot)
        lane_slot = jnp.where(lane // 16 == 2 * i + 1, infos_smem[i, 4, 0], lane_slot)
    row = lax.broadcasted_iota(jnp.int32, (NPROMPT * 16, terms), 0)
    lanes = lax.broadcasted_iota(jnp.int32, (NPROMPT * 16, terms), 1)
    chosen = jnp.logical_and(row // 16 == lane_slot, lax.rem(row, 16) == lax.rem(lanes, 16))
    chosen = jnp.where(chosen, 1.0, 0.0).astype(BF16)

    def after_step(kv):
        after(kv)
        for copy in stores(kv):
            copy.start()

    loop(0, KV, after_step)

    for kv in range(KV):
        for d in FAR_XY:
            other = xy_peer(d)
            wait_bytes(parts.at[kv, other], recv_c.at[kv, other])
        sums = [dot(chosen, parts[kv, :, :, n].reshape(terms, HD)) for n in range(2)]
        for i in range(2 * NPROMPT):
            lo = 8 * i
            pieces[i, kv] = jnp.concatenate([sums[0][lo : lo + 8], sums[1][lo : lo + 8]], 0).astype(BF16)
    for off in FAR_Z8:
        for k in range(2):
            start_d(off, k)

    for n in range(PLANE - 1):
        copy_info(n).wait_send()
        copy_b(n).wait_send()
        for kv in range(KV):
            copy_c(kv, n).wait_send()
    for dz in FAR_Z:
        for other_head in range(HEADS):
            wait_send_a(dz, other_head)
    for kv in range(KV):
        for copy in stores(kv):
            copy.wait()
    loop(0, 16, lambda i: wait_bytes(finals.at[i], recv_d.at[i]))
    for other_head in range(HEADS):
        for kv in range(KV):
            total = finals[DEPTH * other_head, kv].astype(F32)
            for other_z in range(1, DEPTH):
                total = total + finals[DEPTH * other_head + other_z, kv].astype(F32)
            lo = (KV * other_head + kv) * HD
            pkg_ref[:, lo : lo + HD] = total[:8].astype(BF16)
            pvg_ref[:, lo : lo + HD] = total[8:].astype(BF16)
    for off in FAR_Z8:
        for k in range(2):
            wait_send_d(off, k)


def hand_over(*refs):
    sources, targets, held, sem_in, sem_out = refs[:6], refs[6:12], refs[12:18], refs[18], refs[19]
    loads, stores = [], []
    for src, dst, mid in zip(sources, targets, held):
        step = src.shape[0] // 4 if src.shape[0] >= 64 else src.shape[0]
        for lo in range(0, src.shape[0], step):
            rows = pl.ds(lo, step)
            n = len(loads)
            loads.append(pltpu.make_async_copy(src.at[rows], mid.at[rows], sem_in.at[n]))
            stores.append(pltpu.make_async_copy(mid.at[rows], dst.at[rows], sem_out.at[n]))
    for load in loads:
        load.start()
    for load, store in zip(loads, stores):
        load.wait()
        store.start()
    for store in stores:
        store.wait()


def shards(query, comp_key, comp_value, prompt_key, prompt_value, out_grad, row_comp, prompt_owner):
    vmem = pl.BlockSpec(memory_space=pltpu.VMEM)
    smem = pl.BlockSpec(memory_space=pltpu.SMEM)
    hbm = pl.BlockSpec(memory_space=pl.ANY)
    dma = pltpu.SemaphoreType.DMA
    wide_rows = (KV, ROWS, WIDE)
    rows = (KV, ROWS, HD)
    heads_wide = GROUP * ROWS
    prompt_rows = prompt_key.shape
    like = lambda a: jax.ShapeDtypeStruct(a.shape, BF16)
    buf = pltpu.VMEM
    results = pl.pallas_call(
        kernel,
        out_shape=(
            like(query), like(query), like(comp_key), like(comp_value), like(prompt_key), like(prompt_value),
        ),
        in_specs=[hbm] * 8,
        out_specs=(hbm, hbm, hbm, hbm, vmem, vmem),
        scratch_shapes=[
            pltpu.SMEM((NPROMPT,), jnp.int32), pltpu.SMEM((ROWS,), jnp.int32),
            buf(wide_rows, BF16), buf(wide_rows, BF16), buf(rows, BF16), buf(rows, BF16),
            buf(prompt_rows, BF16), buf(prompt_rows, BF16),
            buf((HEADS, KV, 16, HD), BF16),
            buf((16, KV, 16, HD), BF16),
            buf((NPROMPT, KV, 2, 16, HD), BF16),
            buf((PLANE, KV, 2, 2, 16, HD), BF16),
            buf((PLANE, KV, 2, 2, 16, HD), BF16),
            buf((8, 128), jnp.int32),
            buf((PLANE, 8, 128), jnp.int32),
            pltpu.SMEM((PLANE, 8, 128), jnp.int32),
            buf((KV, HD, heads_wide), BF16),
            buf((KV, HD, heads_wide), BF16),
            buf((KV, ROWS, heads_wide), F32),
            buf((KV, ROWS, heads_wide), F32),
            buf((KV, HD, heads_wide), F32),
            buf((KV, 8, heads_wide), F32),
            buf((KV, PLEN, heads_wide), BF16),
            buf((KV, PLEN, heads_wide), BF16),
            buf((KV, ROWS, heads_wide), BF16),
            buf((KV, ROWS, heads_wide), BF16),
            buf((KV, HD, heads_wide), BF16),
            buf((KV, 2 * HD, PLEN), BF16),
            buf((KV, PLANE, 2, 2, 16, HD), BF16),
            buf((KV, PLANE, 2, 2, 16, HD), BF16),
            buf((16, KV, 16, HD), BF16),
            buf((16, KV, 16, HD), BF16),
            buf(wide_rows, BF16), buf(wide_rows, BF16), buf(rows, BF16), buf(rows, BF16),
            dma((12,)), dma((8,)), dma,
            dma((16,)), dma((16,)), dma((PLANE,)), dma((PLANE,)),
            dma((PLANE,)), dma((PLANE,)), dma((KV, PLANE)), dma((KV, PLANE)),
            dma((16,)), dma((16,)),
        ],
        compiler_params=pltpu.CompilerParams(
            collective_id=0, has_side_effects=True, vmem_limit_bytes=56 * 1024 * 1024
        ),
        name="attend",
    )(prompt_owner, row_comp, query, comp_key, comp_value, prompt_key, prompt_value, out_grad)
    return pl.pallas_call(
        hand_over,
        out_shape=tuple(like(r) for r in results),
        in_specs=[hbm] * 6,
        out_specs=(hbm,) * 6,
        scratch_shapes=[buf(r.shape, BF16) for r in results] + [dma((18,)), dma((18,))],
        compiler_params=pltpu.CompilerParams(vmem_limit_bytes=60 * 1024 * 1024),
        name="hand_over",
    )(*results)


def solution(mesh):
    placed = (
        P("seq", "head"),
        P("seq", "head"),
        P("seq", "head"),
        P(("seq", "head"), None),
        P(("seq", "head"), None),
        P("seq", "head"),
        P("seq"),
        P(),
    )
    return jax.shard_map(
        shards,
        mesh=mesh,
        in_specs=placed,
        out_specs=(
            P("seq", "head"),
            P("seq", "head"),
            P("seq", "head"),
            P("seq", "head"),
            P(("seq", "head"), None),
            P(("seq", "head"), None),
        ),
        check_vma=False,
    )
```

time: 62.4 us -> 51.3 us (0.82)
  the two profiles are of different devices: /device:TPU:25 before, /device:TPU:1 now
where the time goes in v3:
time: 51.3 us; the launch traced here: 50.9 us
  Pallas kernels  50.3 us (98%)
  between operations  0.64 us (1%)
    pallas_call x1, Pallas kernels, shards(): pl.pallas_call(kernel, out_shape=(like(query), like(query), like(comp_key...  47.5 us
    pallas_call x1, Pallas kernels, shards(): pl.pallas_call(hand_over, out_shape=tuple((like(r) for r in results)), in...  2.74 us

profile of v3, /device:TPU:1, one launch (start us, length us, event | category | flops | bytes accessed | tf_op | source)
XLA Modules:
  0.0 50.9 jit_solution(15344151356207530259)
XLA Ops:
  0.6 47.5 %attend.1 = (bf16[512,1024]{1,0:T(8,128)(2,1)}, bf16[512,1024]{1,0:T(8,128)(2,1)}, bf16[512,256]{1,0:T(8,128)(2,1)}, bf16[512,256]{1,0:T(8,128)(2,1)}, bf16[8,1024]{1,0:T(8,128)(2,1)}, /*index=5*/bf16[8,1024]{1,0:T(8,128)(2,1)}) custom-call(s32[8]{0:T(128)} %owner_hbm.1, s32[512]{0:T(512)} %comp_hbm.1, bf16[512,1024]{1,0:T(8,128)(2,1)} %q_hbm.1, ...), custom_call_target="tpu_custom_call" | custom-call | tf_op jit(solution)/shard_map/attend/pallas_call | solution.py:510
  48.2 2.7 %hand_over.1 = (bf16[512,1024]{1,0:T(8,128)(2,1)}, bf16[512,1024]{1,0:T(8,128)(2,1)}, bf16[512,256]{1,0:T(8,128)(2,1)}, bf16[512,256]{1,0:T(8,128)(2,1)}, bf16[8...) custom-call(bf16[512,1024]{1,0:T(8,128)(2,1)} %get-tuple-element.12.refs_0_, bf16[512,1024]{1,0:T(8,128)(2,1)} %get-tuple-element.13.refs_1_, ...), custom_call_target="tpu_custom_call" | custom-call | tf_op jit(solution)/shard_map/hand_over/pallas_call | solution.py:556

commit v4 on v3

--- a/solution.py
+++ b/solution.py
@@ -56,12 +56,12 @@
 
 def kernel(
     owner_hbm, comp_hbm, q_hbm, k_hbm, v_hbm, pk_hbm, pv_hbm, g_hbm,
-    out_hbm, qg_hbm, kg_hbm, vg_hbm, pkg_ref, pvg_ref,
+    out_v, qg_v, kg_v, vg_v, finals,
     owner_ref, comp_ref, q_in, g_in, k_in, v_in, pk_in, pv_in,
     own_rows, dense, packed, picked, chosen_kv, info, infos, infos_smem,
     q_turn, g_turn, e_local, p_local, o_local, stats, w_prompt, d_prompt, w_local, d_local, o_turn, pair_turn,
-    part, parts, pieces, finals, out_v, qg_v, kg_v, vg_v,
-    in_sem, out_sem, local_sem, send_a, recv_a, send_i, recv_i, send_b, recv_b, send_c, recv_c, send_d, recv_d,
+    part, parts, pieces,
+    in_sem, local_sem, send_a, recv_a, send_i, recv_i, send_b, recv_b, send_c, recv_c, send_d, recv_d,
 ):
     seq, head, x, y, z, z8, core, slot = place()
     plane = 4 * x + y
@@ -87,16 +87,6 @@
 
     def signal(other, other_head):
         pl.semaphore_signal(barrier, inc=1, device_id=(other, other_head), device_id_type=MESH)
-
-    def greet_spread(dz):
-        for other_head in range(HEADS):
-            other, _ = spread_target(dz, other_head)
-            if dz:
-                signal(other, jnp.int32(other_head))
-            else:
-                @pl.when(jnp.logical_not(jnp.logical_and(own, head == other_head)))
-                def _():
-                    signal(other, jnp.int32(other_head))
 
     def greet_holder(off):
         for k in range(2):
@@ -108,25 +98,20 @@
                 def _():
                     signal(other, other_head)
 
-    greet_spread(2)
-    for off in (4, 3, 5):
-        greet_holder(off)
-    greet_spread(1)
-    greet_spread(3)
-    for off in (2, 6):
-        greet_holder(off)
-    greet_spread(0)
-    for off in (1, 7, 0):
-        greet_holder(off)
-    for d in FAR_XY:
-        signal(xy_peer(d) * DEPTH + z, head)
-
-    loads = [
+    small = [
         pltpu.make_async_copy(pk_hbm, pk_in, in_sem.at[0]),
         pltpu.make_async_copy(pv_hbm, pv_in, in_sem.at[1]),
         pltpu.make_async_copy(owner_hbm, owner_ref, in_sem.at[10]),
         pltpu.make_async_copy(comp_hbm, comp_ref, in_sem.at[11]),
     ]
+    for load in small:
+        load.start()
+    for off in FAR_Z8:
+        greet_holder(off)
+    for d in FAR_XY:
+        signal(xy_peer(d) * DEPTH + z, head)
+
+    loads = []
     for kv in range(KV):
         wide, narrow = pl.ds(kv * WIDE, WIDE), pl.ds(kv * HD, HD)
         for n, (src, dst, cols) in enumerate(
@@ -135,7 +120,7 @@
             loads.append(pltpu.make_async_copy(src.at[:, cols], dst.at[kv], in_sem.at[2 + 4 * kv + n]))
     for load in loads:
         load.start()
-    for load in loads[:4]:
+    for load in small:
         load.wait()
 
     both = jnp.concatenate([pk_in[...].astype(F32), pv_in[...].astype(F32)], 0).astype(BF16)
@@ -152,9 +137,6 @@
         split = jnp.where(comp_ref[split + step - 1] == lead_comp, split + step, split)
     info[...] = jnp.where(lax.broadcasted_iota(jnp.int32, (8, 128), 0) < 4, lead, tail)
     infos[plane] = info[...]
-
-    for load in loads[4:]:
-        load.wait()
 
     def loop(lo, hi, body):
         def step(i, carry):
@@ -209,15 +191,21 @@
         return jnp.concatenate([jnp.where(in_lead, rows, zero), jnp.where(in_lead, zero, rows)], 1)
 
     def middle(kv):
-        key_pair = jnp.concatenate([chosen_kv[:, kv, t, 0].reshape(PLEN, HD) for t in range(2)], 1)
-        value_pair = jnp.concatenate([chosen_kv[:, kv, t, 1].reshape(PLEN, HD) for t in range(2)], 1)
+        key_pair = jnp.concatenate([chosen_kv[kv, :, t, 0].reshape(PLEN, HD) for t in range(2)], 1)
+        value_pair = jnp.concatenate([chosen_kv[kv, :, t, 1].reshape(PLEN, HD) for t in range(2)], 1)
         pair_turn[kv] = key_pair.T
         value_pair_t = value_pair.T
-        for chunk in range(CHUNKS):
-            span = slice(chunk * SPAN, (chunk + 1) * SPAN)
-            is_lead = chunk * CHUNK + lane_row < split
-            g_t = g_turn[kv, :, span]
-            s_prompt = dot(key_pair, pair_of(q_turn[kv, :, span], is_lead))
+        spans = [slice(c * SPAN, (c + 1) * SPAN) for c in range(CHUNKS)]
+        leads = [c * CHUNK + lane_row < split for c in range(CHUNKS)]
+
+        def products(c):
+            return (
+                dot(key_pair, pair_of(q_turn[kv, :, spans[c]], leads[c])),
+                dot(value_pair, pair_of(g_turn[kv, :, spans[c]], leads[c])),
+            )
+
+        def weigh(c, s_prompt):
+            span = spans[c]
             top_local = stats[kv, 0:1, span]
             top = jnp.maximum(top_local, jnp.max(s_prompt, axis=0, keepdims=True))
             e_prompt = jnp.exp2((s_prompt - top) * EXP2_SCALE)
@@ -227,14 +215,30 @@
             e_prompt = e_prompt * inv
             wh_prompt = e_prompt.astype(BF16)
             w_prompt[kv, :, span] = wh_prompt
+            stats[kv, 2:3, span] = rescale
             o_pair = dot(value_pair_t, wh_prompt)
-            o_t = jnp.where(is_lead, o_pair[:HD], o_pair[HD:]) + o_local[kv, :, span] * rescale
+            return e_prompt, o_pair, rescale
+
+        def finish(c, e_prompt, o_pair, rescale, p_prompt):
+            span = spans[c]
+            o_t = jnp.where(leads[c], o_pair[:HD], o_pair[HD:]) + o_local[kv, :, span] * rescale
             o_t = o_t.astype(BF16)
             o_turn[kv, :, span] = o_t
-            delta = jnp.sum(o_t.astype(F32) * g_t.astype(F32), axis=0, keepdims=True)
-            stats[kv, 2:3, span] = rescale
+            delta = jnp.sum(o_t.astype(F32) * g_turn[kv, :, span].astype(F32), axis=0, keepdims=True)
             stats[kv, 3:4, span] = delta
-            d_prompt[kv, :, span] = (e_prompt * (dot(value_pair, pair_of(g_t, is_lead)) - delta)).astype(BF16)
+            d_prompt[kv, :, span] = (e_prompt * (p_prompt - delta)).astype(BF16)
+
+        ahead = products(0)
+        held = None
+        for c in range(CHUNKS):
+            s_prompt, p_prompt = ahead
+            if c + 1 < CHUNKS:
+                ahead = products(c + 1)
+            weighed = weigh(c, s_prompt)
+            if held is not None:
+                finish(*held)
+            held = (c, *weighed, p_prompt)
+        finish(*held)
         dk_pair = dot(d_prompt[kv], stacked_pair(q_in, kv)) * INV_SQRT
         dv_pair = dot(w_prompt[kv], stacked_pair(g_in, kv))
         for t in range(2):
@@ -269,16 +273,6 @@
             kg_v[kv, lo:hi] = (dot(d_local[kv, lo:hi, start:], q_all[start:]) * INV_SQRT).astype(BF16)
             vg_v[kv, lo:hi] = dot(w_local[kv, lo:hi, start:], g_all[start:]).astype(BF16)
 
-    def store(kv, n, src, dst, width):
-        cols = pl.ds(pl.multiple_of(kv * width, width), width)
-        return pltpu.make_async_copy(src.at[kv], dst.at[:, cols], out_sem.at[4 * kv + n])
-
-    def stores(kv):
-        return (
-            store(kv, 0, out_v, out_hbm, WIDE), store(kv, 1, qg_v, qg_hbm, WIDE),
-            store(kv, 2, kg_v, kg_hbm, HD), store(kv, 3, vg_v, vg_hbm, HD),
-        )
-
     def copy_a(dz, other_head):
         at = 2 * slot + core
         return pltpu.make_async_remote_copy(
@@ -319,9 +313,10 @@
             device_id=(xy_peer(FAR_XY[n]) * DEPTH + z, head), device_id_type=MESH,
         )
 
-    def copy_b(n):
+    def copy_b(kv, n):
         return pltpu.make_async_remote_copy(
-            src_ref=picked.at[n], dst_ref=chosen_kv.at[plane], send_sem=send_b.at[n], recv_sem=recv_b.at[plane],
+            src_ref=picked.at[kv, n], dst_ref=chosen_kv.at[kv, plane],
+            send_sem=send_b.at[kv, n], recv_sem=recv_b.at[kv, plane],
             device_id=(xy_peer(FAR_XY[n]) * DEPTH + z, head), device_id_type=MESH,
         )
 
@@ -370,22 +365,22 @@
         def _():
             copy.wait_send()
 
-    before(0)
-
-    @pl.when(own)
+    @pl.when(self_slot)
     def _():
-        pl.semaphore_wait(barrier, 15 + 15 + 15)
-
-    @pl.when(jnp.logical_not(own))
+        pl.semaphore_wait(barrier, 15 + 15)
+
+    @pl.when(jnp.logical_not(self_slot))
     def _():
-        pl.semaphore_wait(barrier, 15 + 16 + 16)
+        pl.semaphore_wait(barrier, 15 + 16)
 
     for dz in FAR_Z:
         for other_head in range(HEADS):
             start_a(dz, other_head)
     for n in range(PLANE - 1):
         copy_info(n).start()
-    before(1)
+    for load in loads:
+        load.wait()
+    loop(0, KV, before)
     for d in FAR_XY:
         other = xy_peer(d)
         wait_bytes(infos.at[other], recv_i.at[other])
@@ -399,22 +394,19 @@
             second = dense[2 * p + 1, kv].astype(F32)
             packed[p, kv, 0] = jnp.concatenate([first[:8], second[:8]], 0).astype(BF16)
             packed[p, kv, 1] = jnp.concatenate([first[8:], second[8:]], 0).astype(BF16)
-    for n, d in enumerate(FAR_XY):
-        other = xy_peer(d)
-        other_lead = infos_smem[other, 0, 0]
-        other_tail = infos_smem[other, 4, 0]
-        for kv in range(KV):
-            picked[n, kv, 0] = packed[other_lead, kv]
-            picked[n, kv, 1] = packed[other_tail, kv]
-        copy_b(n).start()
     for kv in range(KV):
-        chosen_kv[plane, kv, 0] = packed[lead, kv]
-        chosen_kv[plane, kv, 1] = packed[tail, kv]
-    for d in FAR_XY:
-        other = xy_peer(d)
-        wait_bytes(chosen_kv.at[other], recv_b.at[other])
+        for n, d in enumerate(FAR_XY):
+            other = xy_peer(d)
+            picked[kv, n, 0] = packed[infos_smem[other, 0, 0], kv]
+            picked[kv, n, 1] = packed[infos_smem[other, 4, 0], kv]
+            copy_b(kv, n).start()
+        chosen_kv[kv, plane, 0] = packed[lead, kv]
+        chosen_kv[kv, plane, 1] = packed[tail, kv]
 
     def middle_step(kv):
+        for d in FAR_XY:
+            other = xy_peer(d)
+            wait_bytes(chosen_kv.at[kv, other], recv_b.at[kv, other])
         middle(kv)
         for n in range(PLANE - 1):
             copy_c(kv, n).start()
@@ -435,8 +427,6 @@
 
     def after_step(kv):
         after(kv)
-        for copy in stores(kv):
-            copy.start()
 
     loop(0, KV, after_step)
 
@@ -454,16 +444,26 @@
 
     for n in range(PLANE - 1):
         copy_info(n).wait_send()
-        copy_b(n).wait_send()
         for kv in range(KV):
+            copy_b(kv, n).wait_send()
             copy_c(kv, n).wait_send()
     for dz in FAR_Z:
         for other_head in range(HEADS):
             wait_send_a(dz, other_head)
-    for kv in range(KV):
-        for copy in stores(kv):
-            copy.wait()
+    for off in FAR_Z8:
+        for k in range(2):
+            wait_send_d(off, k)
     loop(0, 16, lambda i: wait_bytes(finals.at[i], recv_d.at[i]))
+
+
+def hand_over(out_v, qg_v, kg_v, vg_v, finals, out_hbm, qg_hbm, kg_hbm, vg_hbm, pkg_ref, pvg_ref, sem):
+    copies = []
+    for src, dst, width in ((out_v, out_hbm, WIDE), (qg_v, qg_hbm, WIDE), (kg_v, kg_hbm, HD), (vg_v, vg_hbm, HD)):
+        for kv in range(KV):
+            target = dst.at[:, pl.ds(kv * width, width)]
+            copies.append(pltpu.make_async_copy(src.at[kv], target, sem.at[len(copies)]))
+    for copy in copies:
+        copy.start()
     for other_head in range(HEADS):
         for kv in range(KV):
             total = finals[DEPTH * other_head, kv].astype(F32)
@@ -472,33 +472,12 @@
             lo = (KV * other_head + kv) * HD
             pkg_ref[:, lo : lo + HD] = total[:8].astype(BF16)
             pvg_ref[:, lo : lo + HD] = total[8:].astype(BF16)
-    for off in FAR_Z8:
-        for k in range(2):
-            wait_send_d(off, k)
-
-
-def hand_over(*refs):
-    sources, targets, held, sem_in, sem_out = refs[:6], refs[6:12], refs[12:18], refs[18], refs[19]
-    loads, stores = [], []
-    for src, dst, mid in zip(sources, targets, held):
-        step = src.shape[0] // 4 if src.shape[0] >= 64 else src.shape[0]
-        for lo in range(0, src.shape[0], step):
-            rows = pl.ds(lo, step)
-            n = len(loads)
-            loads.append(pltpu.make_async_copy(src.at[rows], mid.at[rows], sem_in.at[n]))
-            stores.append(pltpu.make_async_copy(mid.at[rows], dst.at[rows], sem_out.at[n]))
-    for load in loads:
-        load.start()
-    for load, store in zip(loads, stores):
-        load.wait()
-        store.start()
-    for store in stores:
-        store.wait()
+    for copy in copies:
+        copy.wait()
 
 
 def shards(query, comp_key, comp_value, prompt_key, prompt_value, out_grad, row_comp, prompt_owner):
     vmem = pl.BlockSpec(memory_space=pltpu.VMEM)
-    smem = pl.BlockSpec(memory_space=pltpu.SMEM)
     hbm = pl.BlockSpec(memory_space=pl.ANY)
     dma = pltpu.SemaphoreType.DMA
     wide_rows = (KV, ROWS, WIDE)
@@ -510,10 +489,11 @@
     results = pl.pallas_call(
         kernel,
         out_shape=(
-            like(query), like(query), like(comp_key), like(comp_value), like(prompt_key), like(prompt_value),
+            buf(wide_rows, BF16), buf(wide_rows, BF16), buf(rows, BF16), buf(rows, BF16),
+            buf((16, KV, 16, HD), BF16),
         ),
         in_specs=[hbm] * 8,
-        out_specs=(hbm, hbm, hbm, hbm, vmem, vmem),
+        out_specs=(vmem,) * 5,
         scratch_shapes=[
             pltpu.SMEM((NPROMPT,), jnp.int32), pltpu.SMEM((ROWS,), jnp.int32),
             buf(wide_rows, BF16), buf(wide_rows, BF16), buf(rows, BF16), buf(rows, BF16),
@@ -521,8 +501,8 @@
             buf((HEADS, KV, 16, HD), BF16),
             buf((16, KV, 16, HD), BF16),
             buf((NPROMPT, KV, 2, 16, HD), BF16),
-            buf((PLANE, KV, 2, 2, 16, HD), BF16),
-            buf((PLANE, KV, 2, 2, 16, HD), BF16),
+            buf((KV, PLANE, 2, 2, 16, HD), BF16),
+            buf((KV, PLANE, 2, 2, 16, HD), BF16),
             buf((8, 128), jnp.int32),
             buf((PLANE, 8, 128), jnp.int32),
             pltpu.SMEM((PLANE, 8, 128), jnp.int32),
@@ -541,11 +521,9 @@
             buf((KV, PLANE, 2, 2, 16, HD), BF16),
             buf((KV, PLANE, 2, 2, 16, HD), BF16),
             buf((16, KV, 16, HD), BF16),
-            buf((16, KV, 16, HD), BF16),
-            buf(wide_rows, BF16), buf(wide_rows, BF16), buf(rows, BF16), buf(rows, BF16),
-            dma((12,)), dma((8,)), dma,
+            dma((12,)), dma,
             dma((16,)), dma((16,)), dma((PLANE,)), dma((PLANE,)),
-            dma((PLANE,)), dma((PLANE,)), dma((KV, PLANE)), dma((KV, PLANE)),
+            dma((KV, PLANE)), dma((KV, PLANE)), dma((KV, PLANE)), dma((KV, PLANE)),
             dma((16,)), dma((16,)),
         ],
         compiler_params=pltpu.CompilerParams(
@@ -555,13 +533,14 @@
     )(prompt_owner, row_comp, query, comp_key, comp_value, prompt_key, prompt_value, out_grad)
     return pl.pallas_call(
         hand_over,
-        out_shape=tuple(like(r) for r in results),
-        in_specs=[hbm] * 6,
-        out_specs=(hbm,) * 6,
-        scratch_shapes=[buf(r.shape, BF16) for r in results] + [dma((18,)), dma((18,))],
-        compiler_params=pltpu.CompilerParams(vmem_limit_bytes=60 * 1024 * 1024),
+        out_shape=(
+            like(query), like(query), like(comp_key), like(comp_value), like(prompt_key), like(prompt_value),
+        ),
+        in_specs=[hbm] * 4 + [vmem],
+        out_specs=(hbm,) * 4 + (vmem, vmem),
+        scratch_shapes=[dma((8,))],
         name="hand_over",
-    )(*results)
+    )(*(pltpu.with_memory_space_constraint(r, pltpu.VMEM) for r in results))
 
 
 def solution(mesh):

time: 51.3 us -> 47.5 us (0.926)
  Pallas kernels: 50.3 us -> 46.4 us
    pallas_call x2, Pallas kernels: 50.3 us -> 46.4 us  [the longest x1 44.2 us: shards(): pl.pallas_call(kernel, out_shape=(buf(wide_rows, BF16), buf(wide_rows, BF...]
where the time goes in v4:
time: 47.5 us; the launch traced here: 47 us
  Pallas kernels  46.4 us (98%)
  between operations  0.64 us (1%)
    pallas_call x1, Pallas kernels, shards(): pl.pallas_call(kernel, out_shape=(buf(wide_rows, BF16), buf(wide_rows, BF...  44.2 us
    pallas_call x1, Pallas kernels, shards(): pl.pallas_call(hand_over, out_shape=(like(query), like(query), like(comp_...  2.16 us

profile of v4, /device:TPU:1, one launch (start us, length us, event | category | flops | bytes accessed | tf_op | source)
XLA Modules:
  0.0 47.0 jit_solution(13879138040781681809)
XLA Ops:
  0.6 44.2 %attend.1 = (bf16[2,512,512]{2,1,0:T(8,128)(2,1)S(1)}, bf16[2,512,512]{2,1,0:T(8,128)(2,1)S(1)}, bf16[2,512,128]{2,1,0:T(8,128)(2,1)S(1)}, bf16[2,512,128]{2,1,0:T(8,128)(2,1)S(1)}, bf16[16,2,16,128]{3,2,1,0:T(8,128)(2,1)S(1)}) custom-call(s32[8]{0:T(128)} %owner_hbm.1, s32[512]{0:T(512)} %comp_hbm.1, bf16[512,1024]{1,0:T(8,128)(2,1)} %q_hbm.1, ...), custom_call_target="tpu_custom_call" | custom-call | tf_op jit(solution)/shard_map/attend/pallas_call | solution.py:489
  44.9 2.2 %hand_over.1 = (bf16[512,1024]{1,0:T(8,128)(2,1)}, bf16[512,1024]{1,0:T(8,128)(2,1)}, bf16[512,256]{1,0:T(8,128)(2,1)}, bf16[512,256]{1,0:T(8,128)(2,1)}, bf16[8...) custom-call(bf16[2,512,512]{2,1,0:T(8,128)(2,1)S(1)} %get-tuple-element.11.out_v, ...), custom_call_target="tpu_custom_call" | custom-call | tf_op jit(solution)/shard_map/hand_over/pallas_call | solution.py:534

commit v5 on v4

--- a/solution.py
+++ b/solution.py
@@ -59,7 +59,7 @@
     out_v, qg_v, kg_v, vg_v, finals,
     owner_ref, comp_ref, q_in, g_in, k_in, v_in, pk_in, pv_in,
     own_rows, dense, packed, picked, chosen_kv, info, infos, infos_smem,
-    q_turn, g_turn, e_local, p_local, o_local, stats, w_prompt, d_prompt, w_local, d_local, o_turn, pair_turn,
+    q_pair_turn, g_pair_turn, q_pair, g_pair, e_local, p_local, o_local, stats, w_prompt, d_prompt, w_local, d_local, key_pair_turn, value_pair_turn,
     part, parts, pieces,
     in_sem, local_sem, send_a, recv_a, send_i, recv_i, send_b, recv_b, send_c, recv_c, send_d, recv_d,
 ):
@@ -147,6 +147,10 @@
 
     lane_row = lax.broadcasted_iota(jnp.int32, (1, SPAN), 1) % CHUNK
 
+    def pair_of(turned, is_lead):
+        zero = jnp.zeros_like(turned)
+        return jnp.concatenate([jnp.where(is_lead, turned, zero), jnp.where(is_lead, zero, turned)], 0)
+
     def before(kv):
         values_t = v_in[kv].T
         for chunk in range(CHUNKS):
@@ -154,8 +158,18 @@
             span = slice(chunk * SPAN, (chunk + 1) * SPAN)
             q_t = jnp.concatenate([q_in[kv, lo:hi, j * HD : (j + 1) * HD].T for j in range(GROUP)], 1)
             g_t = jnp.concatenate([g_in[kv, lo:hi, j * HD : (j + 1) * HD].T for j in range(GROUP)], 1)
-            q_turn[kv, :, span] = q_t
-            g_turn[kv, :, span] = g_t
+            is_lead = lo + lane_row < split
+            q_pair_turn[kv, :, span] = pair_of(q_t, is_lead)
+            g_pair_turn[kv, :, span] = pair_of(g_t, is_lead)
+            lead_rows = lo + lax.broadcasted_iota(jnp.int32, (CHUNK, HD), 0) < split
+            lead_rows = jnp.where(lead_rows, 1.0, 0.0).astype(BF16)
+            for j in range(GROUP):
+                at = slice(chunk * SPAN + j * CHUNK, chunk * SPAN + (j + 1) * CHUNK)
+                for src, dst in ((q_in, q_pair), (g_in, g_pair)):
+                    block = src[kv, lo:hi, j * HD : (j + 1) * HD]
+                    in_lead = block * lead_rows
+                    dst[kv, at, :HD] = in_lead
+                    dst[kv, at, HD:] = block - in_lead
             key_at = lax.broadcasted_iota(jnp.int32, (hi, CHUNK), 0)
             row_at = lo + lax.broadcasted_iota(jnp.int32, (hi, CHUNK), 1)
             seen = jnp.logical_and(key_at <= row_at, jnp.logical_or(key_at >= split, row_at < split))
@@ -167,11 +181,9 @@
             o_local[kv, :, span] = dot(values_t[:, :hi], raw.astype(BF16))
             stats[kv, 0:1, span] = top
             stats[kv, 1:2, span] = jnp.sum(raw, axis=0, keepdims=True)
-            p_local[kv, :hi, span] = dot(v_in[kv, :hi], g_t)
-
-    def pair_of(turned, is_lead):
-        zero = jnp.zeros_like(turned)
-        return jnp.concatenate([jnp.where(is_lead, turned, zero), jnp.where(is_lead, zero, turned)], 0)
+            grads = dot(v_in[kv, :hi], g_t)
+            p_local[kv, :hi, span] = grads
+            stats[kv, 4:5, span] = jnp.sum(raw * grads, axis=0, keepdims=True)
 
     def stacked(ref, kv):
         return jnp.concatenate(
@@ -183,64 +195,47 @@
             0,
         )
 
-    def stacked_pair(ref, kv):
-        rows = stacked(ref, kv)
-        at = lax.broadcasted_iota(jnp.int32, (GROUP * ROWS, 1), 0)
-        in_lead = (at // SPAN) * CHUNK + at % CHUNK < split
-        zero = jnp.zeros_like(rows)
-        return jnp.concatenate([jnp.where(in_lead, rows, zero), jnp.where(in_lead, zero, rows)], 1)
-
     def middle(kv):
         key_pair = jnp.concatenate([chosen_kv[kv, :, t, 0].reshape(PLEN, HD) for t in range(2)], 1)
         value_pair = jnp.concatenate([chosen_kv[kv, :, t, 1].reshape(PLEN, HD) for t in range(2)], 1)
-        pair_turn[kv] = key_pair.T
-        value_pair_t = value_pair.T
+        key_pair_turn[kv] = key_pair.T
+        value_pair_turn[kv] = value_pair.T
         spans = [slice(c * SPAN, (c + 1) * SPAN) for c in range(CHUNKS)]
-        leads = [c * CHUNK + lane_row < split for c in range(CHUNKS)]
 
         def products(c):
             return (
-                dot(key_pair, pair_of(q_turn[kv, :, spans[c]], leads[c])),
-                dot(value_pair, pair_of(g_turn[kv, :, spans[c]], leads[c])),
+                dot(key_pair, q_pair_turn[kv, :, spans[c]]),
+                dot(value_pair, g_pair_turn[kv, :, spans[c]]),
             )
 
-        def weigh(c, s_prompt):
+        def weigh(c, s_prompt, p_prompt):
             span = spans[c]
             top_local = stats[kv, 0:1, span]
             top = jnp.maximum(top_local, jnp.max(s_prompt, axis=0, keepdims=True))
-            e_prompt = jnp.exp2((s_prompt - top) * EXP2_SCALE)
+            raw = jnp.exp2((s_prompt - top) * EXP2_SCALE)
             rescale = jnp.exp2((top_local - top) * EXP2_SCALE)
-            inv = 1.0 / (jnp.sum(e_prompt, axis=0, keepdims=True) + rescale * stats[kv, 1:2, span])
-            rescale = rescale * inv
-            e_prompt = e_prompt * inv
-            wh_prompt = e_prompt.astype(BF16)
-            w_prompt[kv, :, span] = wh_prompt
-            stats[kv, 2:3, span] = rescale
-            o_pair = dot(value_pair_t, wh_prompt)
-            return e_prompt, o_pair, rescale
-
-        def finish(c, e_prompt, o_pair, rescale, p_prompt):
-            span = spans[c]
-            o_t = jnp.where(leads[c], o_pair[:HD], o_pair[HD:]) + o_local[kv, :, span] * rescale
-            o_t = o_t.astype(BF16)
-            o_turn[kv, :, span] = o_t
-            delta = jnp.sum(o_t.astype(F32) * g_turn[kv, :, span].astype(F32), axis=0, keepdims=True)
+            inv = 1.0 / (jnp.sum(raw, axis=0, keepdims=True) + rescale * stats[kv, 1:2, span])
+            delta = jnp.sum(raw * p_prompt, axis=0, keepdims=True) + rescale * stats[kv, 4:5, span]
+            delta = delta * inv
+            weights = raw * inv
+            w_prompt[kv, :, span] = weights.astype(BF16)
+            d_prompt[kv, :, span] = (weights * (p_prompt - delta)).astype(BF16)
+            stats[kv, 2:3, span] = rescale * inv
             stats[kv, 3:4, span] = delta
-            d_prompt[kv, :, span] = (e_prompt * (p_prompt - delta)).astype(BF16)
-
+
+        half = GROUP * ROWS // 2
         ahead = products(0)
-        held = None
+        dk_pair = dv_pair = 0.0
         for c in range(CHUNKS):
-            s_prompt, p_prompt = ahead
+            now = ahead
             if c + 1 < CHUNKS:
                 ahead = products(c + 1)
-            weighed = weigh(c, s_prompt)
-            if held is not None:
-                finish(*held)
-            held = (c, *weighed, p_prompt)
-        finish(*held)
-        dk_pair = dot(d_prompt[kv], stacked_pair(q_in, kv)) * INV_SQRT
-        dv_pair = dot(w_prompt[kv], stacked_pair(g_in, kv))
+            weigh(c, *now)
+            if c % 2:
+                at = slice((c // 2) * half, (c // 2 + 1) * half)
+                dv_pair += dot(w_prompt[kv, :, at], g_pair[kv, at])
+                dk_pair += dot(d_prompt[kv, :, at], q_pair[kv, at])
+        dk_pair = dk_pair * INV_SQRT
         for t in range(2):
             part[kv, :, t, 0] = dk_pair[:, t * HD : (t + 1) * HD].astype(BF16).reshape(PLANE, 16, HD)
             part[kv, :, t, 1] = dv_pair[:, t * HD : (t + 1) * HD].astype(BF16).reshape(PLANE, 16, HD)
@@ -257,10 +252,12 @@
             w_local[kv, :hi, span] = weights.astype(BF16)
             ds_local = (weights * (p_local[kv, :hi, span] - delta)).astype(BF16)
             d_local[kv, :hi, span] = ds_local
-            dq_pair = dot(pair_turn[kv], d_prompt[kv, :, span])
+            dq_pair = dot(key_pair_turn[kv], d_prompt[kv, :, span])
             dq_t = jnp.where(is_lead, dq_pair[:HD], dq_pair[HD:]) + dot(keys_t[:, :hi], ds_local)
             dq_t = (dq_t * INV_SQRT).astype(BF16)
-            o_t = o_turn[kv, :, span]
+            o_pair = dot(value_pair_turn[kv], w_prompt[kv, :, span])
+            o_t = jnp.where(is_lead, o_pair[:HD], o_pair[HD:]) + o_local[kv, :, span] * rescale
+            o_t = o_t.astype(BF16)
             for j in range(GROUP):
                 cols = slice(j * HD, (j + 1) * HD)
                 out_v[kv, lo:hi, cols] = o_t[:, j * CHUNK : (j + 1) * CHUNK].T
@@ -386,8 +383,20 @@
         wait_bytes(infos.at[other], recv_i.at[other])
     to_smem = pltpu.make_async_copy(infos, infos_smem, local_sem)
     to_smem.start()
+    to_smem.wait()
+
+    terms = 2 * PLANE * 16
+    lane = lax.broadcasted_iota(jnp.int32, (1, terms), 1)
+    lane_slot = jnp.zeros((1, terms), jnp.int32)
+    for i in range(PLANE):
+        lane_slot = jnp.where(lane // 16 == 2 * i, infos_smem[i, 0, 0], lane_slot)
+        lane_slot = jnp.where(lane // 16 == 2 * i + 1, infos_smem[i, 4, 0], lane_slot)
+    row = lax.broadcasted_iota(jnp.int32, (NPROMPT * 16, terms), 0)
+    lanes = lax.broadcasted_iota(jnp.int32, (NPROMPT * 16, terms), 1)
+    chosen = jnp.logical_and(row // 16 == lane_slot, lax.rem(row, 16) == lax.rem(lanes, 16))
+    chosen = jnp.where(chosen, 1.0, 0.0).astype(BF16)
+
     loop(0, 16, lambda i: wait_bytes(dense.at[i], recv_a.at[i]))
-    to_smem.wait()
     for p in range(NPROMPT):
         for kv in range(KV):
             first = dense[2 * p, kv].astype(F32)
@@ -414,17 +423,6 @@
 
     loop(0, KV, middle_step)
 
-    terms = 2 * PLANE * 16
-    lane = lax.broadcasted_iota(jnp.int32, (1, terms), 1)
-    lane_slot = jnp.zeros((1, terms), jnp.int32)
-    for i in range(PLANE):
-        lane_slot = jnp.where(lane // 16 == 2 * i, infos_smem[i, 0, 0], lane_slot)
-        lane_slot = jnp.where(lane // 16 == 2 * i + 1, infos_smem[i, 4, 0], lane_slot)
-    row = lax.broadcasted_iota(jnp.int32, (NPROMPT * 16, terms), 0)
-    lanes = lax.broadcasted_iota(jnp.int32, (NPROMPT * 16, terms), 1)
-    chosen = jnp.logical_and(row // 16 == lane_slot, lax.rem(row, 16) == lax.rem(lanes, 16))
-    chosen = jnp.where(chosen, 1.0, 0.0).astype(BF16)
-
     def after_step(kv):
         after(kv)
 
@@ -456,7 +454,7 @@
     loop(0, 16, lambda i: wait_bytes(finals.at[i], recv_d.at[i]))
 
 
-def hand_over(out_v, qg_v, kg_v, vg_v, finals, out_hbm, qg_hbm, kg_hbm, vg_hbm, pkg_ref, pvg_ref, sem):
+def hand_over(out_v, qg_v, kg_v, vg_v, finals, out_hbm, qg_hbm, kg_hbm, vg_hbm, pkg_hbm, pvg_hbm, pkg_v, pvg_v, sem):
     copies = []
     for src, dst, width in ((out_v, out_hbm, WIDE), (qg_v, qg_hbm, WIDE), (kg_v, kg_hbm, HD), (vg_v, vg_hbm, HD)):
         for kv in range(KV):
@@ -470,8 +468,11 @@
             for other_z in range(1, DEPTH):
                 total = total + finals[DEPTH * other_head + other_z, kv].astype(F32)
             lo = (KV * other_head + kv) * HD
-            pkg_ref[:, lo : lo + HD] = total[:8].astype(BF16)
-            pvg_ref[:, lo : lo + HD] = total[8:].astype(BF16)
+            pkg_v[:, lo : lo + HD] = total[:8].astype(BF16)
+            pvg_v[:, lo : lo + HD] = total[8:].astype(BF16)
+    for src, dst in ((pkg_v, pkg_hbm), (pvg_v, pvg_hbm)):
+        copies.append(pltpu.make_async_copy(src, dst, sem.at[len(copies)]))
+        copies[-1].start()
     for copy in copies:
         copy.wait()
 
@@ -506,8 +507,10 @@
             buf((8, 128), jnp.int32),
             buf((PLANE, 8, 128), jnp.int32),
             pltpu.SMEM((PLANE, 8, 128), jnp.int32),
-            buf((KV, HD, heads_wide), BF16),
-            buf((KV, HD, heads_wide), BF16),
+            buf((KV, 2 * HD, heads_wide), BF16),
+            buf((KV, 2 * HD, heads_wide), BF16),
+            buf((KV, heads_wide, 2 * HD), BF16),
+            buf((KV, heads_wide, 2 * HD), BF16),
             buf((KV, ROWS, heads_wide), F32),
             buf((KV, ROWS, heads_wide), F32),
             buf((KV, HD, heads_wide), F32),
@@ -516,7 +519,7 @@
             buf((KV, PLEN, heads_wide), BF16),
             buf((KV, ROWS, heads_wide), BF16),
             buf((KV, ROWS, heads_wide), BF16),
-            buf((KV, HD, heads_wide), BF16),
+            buf((KV, 2 * HD, PLEN), BF16),
             buf((KV, 2 * HD, PLEN), BF16),
             buf((KV, PLANE, 2, 2, 16, HD), BF16),
             buf((KV, PLANE, 2, 2, 16, HD), BF16),
@@ -537,8 +540,8 @@
             like(query), like(query), like(comp_key), like(comp_value), like(prompt_key), like(prompt_value),
         ),
         in_specs=[hbm] * 4 + [vmem],
-        out_specs=(hbm,) * 4 + (vmem, vmem),
-        scratch_shapes=[dma((8,))],
+        out_specs=(hbm,) * 6,
+        scratch_shapes=[buf(prompt_rows, BF16), buf(prompt_rows, BF16), dma((10,))],
         name="hand_over",
     )(*(pltpu.with_memory_space_constraint(r, pltpu.VMEM) for r in results))
 

time: 47.5 us -> 46.2 us (0.973)
  Pallas kernels: 46.4 us -> 45.3 us
    pallas_call x1, Pallas kernels: 2.16 us -> 1.57 us  [shards(): pl.pallas_call(hand_over, out_shape=(like(query), like(query), like(comp_...]
    pallas_call x1, Pallas kernels: 44.2 us -> 43.7 us  [shards(): pl.pallas_call(kernel, out_shape=(buf(wide_rows, BF16), buf(wide_rows, BF...]
where the time goes in v5:
time: 46.2 us; the launch traced here: 45.9 us
  Pallas kernels  45.3 us (98%)
  between operations  0.64 us (1%)
    pallas_call x1, Pallas kernels, shards(): pl.pallas_call(kernel, out_shape=(buf(wide_rows, BF16), buf(wide_rows, BF...  43.7 us
    pallas_call x1, Pallas kernels, shards(): pl.pallas_call(hand_over, out_shape=(like(query), like(query), like(comp_...  1.57 us

profile of v5, /device:TPU:1, one launch (start us, length us, event | category | flops | bytes accessed | tf_op | source)
XLA Modules:
  0.0 45.9 jit_solution(1748007944006021987)
XLA Ops:
  0.6 43.7 %attend.1 = (bf16[2,512,512]{2,1,0:T(8,128)(2,1)S(1)}, bf16[2,512,512]{2,1,0:T(8,128)(2,1)S(1)}, bf16[2,512,128]{2,1,0:T(8,128)(2,1)S(1)}, bf16[2,512,128]{2,1,0:T(8,128)(2,1)S(1)}, bf16[16,2,16,128]{3,2,1,0:T(8,128)(2,1)S(1)}) custom-call(s32[8]{0:T(128)} %owner_hbm.1, s32[512]{0:T(512)} %comp_hbm.1, bf16[512,1024]{1,0:T(8,128)(2,1)} %q_hbm.1, ...), custom_call_target="tpu_custom_call" | custom-call | tf_op jit(solution)/shard_map/attend/pallas_call | solution.py:490
  44.4 1.6 %hand_over.1 = (bf16[512,1024]{1,0:T(8,128)(2,1)}, bf16[512,1024]{1,0:T(8,128)(2,1)}, bf16[512,256]{1,0:T(8,128)(2,1)}, bf16[512,256]{1,0:T(8,128)(2,1)}, bf16[8...) custom-call(bf16[2,512,512]{2,1,0:T(8,128)(2,1)S(1)} %get-tuple-element.11.out_v, ...), custom_call_target="tpu_custom_call" | custom-call | tf_op jit(solution)/shard_map/hand_over/pallas_call | solution.py:537

commit v6 on v5

--- a/solution.py
+++ b/solution.py
@@ -104,10 +104,10 @@
         pltpu.make_async_copy(owner_hbm, owner_ref, in_sem.at[10]),
         pltpu.make_async_copy(comp_hbm, comp_ref, in_sem.at[11]),
     ]
+    for off in FAR_Z8:
+        greet_holder(off)
     for load in small:
         load.start()
-    for off in FAR_Z8:
-        greet_holder(off)
     for d in FAR_XY:
         signal(xy_peer(d) * DEPTH + z, head)
 
@@ -274,7 +274,7 @@
         at = 2 * slot + core
         return pltpu.make_async_remote_copy(
             src_ref=own_rows.at[other_head], dst_ref=dense.at[at],
-            send_sem=send_a.at[4 * dz + other_head], recv_sem=recv_a.at[at],
+            send_sem=send_a.at[4 * dz + other_head], recv_sem=recv_a,
             device_id=spread_target(dz, other_head), device_id_type=MESH,
         )
 
@@ -289,7 +289,7 @@
 
         @pl.when(self_a(other_head))
         def _():
-            pltpu.make_async_copy(own_rows.at[other_head], dense.at[at], recv_a.at[at]).start()
+            pltpu.make_async_copy(own_rows.at[other_head], dense.at[at], recv_a).start()
 
         @pl.when(jnp.logical_not(self_a(other_head)))
         def _():
@@ -306,14 +306,14 @@
 
     def copy_info(n):
         return pltpu.make_async_remote_copy(
-            src_ref=info, dst_ref=infos.at[plane], send_sem=send_i.at[n], recv_sem=recv_i.at[plane],
+            src_ref=info, dst_ref=infos.at[plane], send_sem=send_i.at[n], recv_sem=recv_i,
             device_id=(xy_peer(FAR_XY[n]) * DEPTH + z, head), device_id_type=MESH,
         )
 
     def copy_b(kv, n):
         return pltpu.make_async_remote_copy(
             src_ref=picked.at[kv, n], dst_ref=chosen_kv.at[kv, plane],
-            send_sem=send_b.at[kv, n], recv_sem=recv_b.at[kv, plane],
+            send_sem=send_b.at[kv, n], recv_sem=recv_b.at[kv],
             device_id=(xy_peer(FAR_XY[n]) * DEPTH + z, head), device_id_type=MESH,
         )
 
@@ -321,7 +321,7 @@
         other = xy_peer(FAR_XY[n])
         return pltpu.make_async_remote_copy(
             src_ref=part.at[kv, other], dst_ref=parts.at[kv, plane],
-            send_sem=send_c.at[kv, n], recv_sem=recv_c.at[kv, plane],
+            send_sem=send_c.at[kv, n], recv_sem=recv_c.at[kv],
             device_id=(other * DEPTH + z, head), device_id_type=MESH,
         )
 
@@ -330,7 +330,7 @@
         at = DEPTH * head + z
         return other_slot, pltpu.make_async_remote_copy(
             src_ref=pieces.at[2 * other_slot + k], dst_ref=finals.at[at],
-            send_sem=send_d.at[2 * off + k], recv_sem=recv_d.at[at],
+            send_sem=send_d.at[2 * off + k], recv_sem=recv_d,
             device_id=(other, other_head), device_id_type=MESH,
         )
 
@@ -346,7 +346,7 @@
 
         @pl.when(self_d(k))
         def _():
-            pltpu.make_async_copy(pieces.at[2 * other_slot + k], finals.at[at], recv_d.at[at]).start()
+            pltpu.make_async_copy(pieces.at[2 * other_slot + k], finals.at[at], recv_d).start()
 
         @pl.when(jnp.logical_not(self_d(k)))
         def _():
@@ -378,9 +378,7 @@
     for load in loads:
         load.wait()
     loop(0, KV, before)
-    for d in FAR_XY:
-        other = xy_peer(d)
-        wait_bytes(infos.at[other], recv_i.at[other])
+    wait_bytes(infos.at[pl.ds(0, PLANE - 1)], recv_i)
     to_smem = pltpu.make_async_copy(infos, infos_smem, local_sem)
     to_smem.start()
     to_smem.wait()
@@ -396,7 +394,7 @@
     chosen = jnp.logical_and(row // 16 == lane_slot, lax.rem(row, 16) == lax.rem(lanes, 16))
     chosen = jnp.where(chosen, 1.0, 0.0).astype(BF16)
 
-    loop(0, 16, lambda i: wait_bytes(dense.at[i], recv_a.at[i]))
+    wait_bytes(dense, recv_a)
     for p in range(NPROMPT):
         for kv in range(KV):
             first = dense[2 * p, kv].astype(F32)
@@ -413,9 +411,7 @@
         chosen_kv[kv, plane, 1] = packed[tail, kv]
 
     def middle_step(kv):
-        for d in FAR_XY:
-            other = xy_peer(d)
-            wait_bytes(chosen_kv.at[kv, other], recv_b.at[kv, other])
+        wait_bytes(chosen_kv.at[kv, pl.ds(0, PLANE - 1)], recv_b.at[kv])
         middle(kv)
         for n in range(PLANE - 1):
             copy_c(kv, n).start()
@@ -429,9 +425,7 @@
     loop(0, KV, after_step)
 
     for kv in range(KV):
-        for d in FAR_XY:
-            other = xy_peer(d)
-            wait_bytes(parts.at[kv, other], recv_c.at[kv, other])
+        wait_bytes(parts.at[kv, pl.ds(0, PLANE - 1)], recv_c.at[kv])
         sums = [dot(chosen, parts[kv, :, :, n].reshape(terms, HD)) for n in range(2)]
         for i in range(2 * NPROMPT):
             lo = 8 * i
@@ -451,7 +445,7 @@
     for off in FAR_Z8:
         for k in range(2):
             wait_send_d(off, k)
-    loop(0, 16, lambda i: wait_bytes(finals.at[i], recv_d.at[i]))
+    wait_bytes(finals, recv_d)
 
 
 def hand_over(out_v, qg_v, kg_v, vg_v, finals, out_hbm, qg_hbm, kg_hbm, vg_hbm, pkg_hbm, pvg_hbm, pkg_v, pvg_v, sem):
@@ -525,9 +519,9 @@
             buf((KV, PLANE, 2, 2, 16, HD), BF16),
             buf((16, KV, 16, HD), BF16),
             dma((12,)), dma,
-            dma((16,)), dma((16,)), dma((PLANE,)), dma((PLANE,)),
-            dma((KV, PLANE)), dma((KV, PLANE)), dma((KV, PLANE)), dma((KV, PLANE)),
-            dma((16,)), dma((16,)),
+            dma((16,)), dma, dma((PLANE,)), dma,
+            dma((KV, PLANE)), dma((KV,)), dma((KV, PLANE)), dma((KV,)),
+            dma((16,)), dma,
         ],
         compiler_params=pltpu.CompilerParams(
             collective_id=0, has_side_effects=True, vmem_limit_bytes=56 * 1024 * 1024

time: 46.2 us -> 45.1 us (0.976)
  Pallas kernels: 45.3 us -> 44.1 us
    pallas_call x1, Pallas kernels: 43.7 us -> 42.6 us  [shards(): pl.pallas_call(kernel, out_shape=(buf(wide_rows, BF16), buf(wide_rows, BF...]
where the time goes in v6:
time: 45.1 us; the launch traced here: 44.8 us
  Pallas kernels  44.1 us (98%)
  between operations  0.64 us (1%)
    pallas_call x1, Pallas kernels, shards(): pl.pallas_call(kernel, out_shape=(buf(wide_rows, BF16), buf(wide_rows, BF...  42.6 us
    pallas_call x1, Pallas kernels, shards(): pl.pallas_call(hand_over, out_shape=(like(query), like(query), like(comp_...  1.57 us

profile of v6, /device:TPU:1, one launch (start us, length us, event | category | flops | bytes accessed | tf_op | source)
XLA Modules:
  0.0 44.8 jit_solution(11309717533894262270)
XLA Ops:
  0.6 42.6 %attend.1 = (bf16[2,512,512]{2,1,0:T(8,128)(2,1)S(1)}, bf16[2,512,512]{2,1,0:T(8,128)(2,1)S(1)}, bf16[2,512,128]{2,1,0:T(8,128)(2,1)S(1)}, bf16[2,512,128]{2,1,0:T(8,128)(2,1)S(1)}, bf16[16,2,16,128]{3,2,1,0:T(8,128)(2,1)S(1)}) custom-call(s32[8]{0:T(128)} %owner_hbm.1, s32[512]{0:T(512)} %comp_hbm.1, bf16[512,1024]{1,0:T(8,128)(2,1)} %q_hbm.1, ...), custom_call_target="tpu_custom_call" | custom-call | tf_op jit(solution)/shard_map/attend/pallas_call | solution.py:484
  43.2 1.6 %hand_over.1 = (bf16[512,1024]{1,0:T(8,128)(2,1)}, bf16[512,1024]{1,0:T(8,128)(2,1)}, bf16[512,256]{1,0:T(8,128)(2,1)}, bf16[512,256]{1,0:T(8,128)(2,1)}, bf16[8...) custom-call(bf16[2,512,512]{2,1,0:T(8,128)(2,1)S(1)} %get-tuple-element.11.out_v, ...), custom_call_target="tpu_custom_call" | custom-call | tf_op jit(solution)/shard_map/hand_over/pallas_call | solution.py:531
